TPU v7x, 512 devices: a whole 4x4x16 slice. The times are simulated.
512 devices in a mesh: tensor: 8 (over x, core), context: 64 (over z, y).
Axes of the slice: x: 4, y: 4, z: 16, core: 2. Of those that a mesh axis runs over, the one named last changes fastest.
Arguments:
- features: bfloat16 [3, 8192, 4096], P(None, 'context', 'tensor'), may hold values from -6 to 6
- short_filter: float32 [3, 3, 4096], P(None, None, 'tensor'), may hold values from -3 to 3
- long_filter: bfloat16 [8192, 4096], P('context', 'tensor'), may hold values from -1 to 1
- skip_gain: float32 [4096], P('tensor'), may hold values from -4 to 4
- norm_gain: float32 [4096], P('tensor'), may hold values from 0.1 to 1.9
- out_grad: bfloat16 [8192, 4096], P('context', 'tensor'), may hold values from -6 to 6
Outputs:
- layer_out: bfloat16 [8192, 4096], P('context', 'tensor')
- feature_grad: float32 [3, 8192, 4096], P(None, 'context', 'tensor')
- filter_grad: float32 [8192, 4096], P('context', 'tensor')
All inputs are finite; a program needn't handle non-finite values.
Results may differ from a plain program's by a relative error of at most 0.005.
Values sent between devices are 32-bit elements; how exact they have to be, the bound alone decides.
A program may use at most 64 MiB of HBM per device.

v0:
```python
import math

import jax
import jax.numpy as jnp
from jax import lax
from jax.sharding import PartitionSpec as P

CHANNELS = 4096


eps = 1e-06
exact_mode = lax.Precision.HIGHEST


def shifted(shard, axis, by):
    size = lax.axis_size(axis)
    pairs = [(i, i + by) for i in range(size) if 0 <= i + by < size]
    return lax.ppermute(shard, axis, pairs)


def rounded_copy(values):
    return lax.optimization_barrier(values.astype(jnp.bfloat16)).astype(jnp.float32)


def rotation(left_index, right_index, length, direction):
    product = left_index[:, None] * right_index[None, :] % length
    angles = product.astype(jnp.float32) * (direction * 2.0 * math.pi / length)
    return (jnp.cos(angles), jnp.sin(angles))


def contract(matrix, values, pattern):
    return jnp.einsum(
        pattern, matrix, values, precision=exact_mode, preferred_element_type=jnp.float32
    )


def to_columns(blocks):
    return lax.all_to_all(blocks, "context", split_axis=2, concat_axis=1, tiled=True)


def to_rows(blocks):
    return lax.all_to_all(blocks, "context", split_axis=1, concat_axis=2, tiled=True)


def neighbour_rows(block, direction):
    return shifted(block, "context", direction)


def channel_total(values):
    return lax.psum(jnp.sum(values, axis=-1), "tensor")


def spectrum(columns, rows_here):
    devices = lax.axis_size("context")
    window = rows_here // devices
    doubled = 2 * devices
    length = doubled * rows_here
    my_index = lax.axis_index("context")
    freq_first = jnp.arange(doubled, dtype=jnp.int32)
    cos_first, sin_first = rotation(freq_first, jnp.arange(devices, dtype=jnp.int32), doubled, -1.0)
    first_real = contract(cos_first, columns, "ka,mabc->mkbc")
    first_imag = contract(sin_first, columns, "ka,mabc->mkbc")
    local_rows = my_index * window + jnp.arange(window, dtype=jnp.int32)
    cos_twist, sin_twist = rotation(freq_first, local_rows, length, -1.0)
    cos_twist = cos_twist[None, :, :, None]
    sin_twist = sin_twist[None, :, :, None]
    twist_real = first_real * cos_twist - first_imag * sin_twist
    twist_imag = first_real * sin_twist + first_imag * cos_twist
    count_sig = first_real.shape[0]
    arrived = to_rows(jnp.concatenate([twist_real, twist_imag], axis=0))
    arrived_real = arrived[:count_sig]
    arrived_imag = arrived[count_sig:]
    rows_all = jnp.arange(rows_here, dtype=jnp.int32)
    cos_second, sin_second = rotation(rows_all, rows_all, rows_here, -1.0)
    out_real = contract(cos_second, arrived_real, "nb,mlbc->mlnc") - contract(
        sin_second, arrived_imag, "nb,mlbc->mlnc"
    )
    out_imag = contract(sin_second, arrived_real, "nb,mlbc->mlnc") + contract(
        cos_second, arrived_imag, "nb,mlbc->mlnc"
    )
    return (out_real, out_imag)


def transform(fields, rows_here):
    columns = to_columns(fields[:, None])
    return spectrum(columns, rows_here)


def restore(spec_real, spec_imag, rows_here):
    devices = lax.axis_size("context")
    doubled = 2 * devices
    length = doubled * rows_here
    my_index = lax.axis_index("context")
    rows_all = jnp.arange(rows_here, dtype=jnp.int32)
    cos_second, sin_second = rotation(rows_all, rows_all, rows_here, 1.0)
    back_real = contract(cos_second, spec_real, "bn,mlnc->mlbc") - contract(
        sin_second, spec_imag, "bn,mlnc->mlbc"
    )
    back_imag = contract(sin_second, spec_real, "bn,mlnc->mlbc") + contract(
        cos_second, spec_imag, "bn,mlnc->mlbc"
    )
    freq_local = my_index * 2 + jnp.arange(2, dtype=jnp.int32)
    cos_twist, sin_twist = rotation(freq_local, rows_all, length, 1.0)
    cos_twist = cos_twist[None, :, :, None]
    sin_twist = sin_twist[None, :, :, None]
    twist_real = back_real * cos_twist - back_imag * sin_twist
    twist_imag = back_real * sin_twist + back_imag * cos_twist
    count_sig = spec_real.shape[0]
    arrived = to_columns(jnp.concatenate([twist_real, twist_imag], axis=0))
    arrived_real = arrived[:count_sig]
    arrived_imag = arrived[count_sig:]
    cos_first, sin_first = rotation(
        jnp.arange(devices, dtype=jnp.int32), jnp.arange(doubled, dtype=jnp.int32), doubled, 1.0
    )
    signal_real = (
        contract(cos_first, arrived_real, "ak,mkbc->mabc")
        - contract(sin_first, arrived_imag, "ak,mkbc->mabc")
    ) / length
    return to_rows(signal_real)[:, 0]


def backward_pair(back_real, back_imag, lag_real, lag_imag, rows_here):
    both = restore(jnp.stack([back_real, lag_real]), jnp.stack([back_imag, lag_imag]), rows_here)
    return (both[0], both[1])


def layer_core(queries, key_part, value_part, filters, incoming, skip_gain, norm_gain, rows_here):
    mixed = rounded_copy(key_part * value_part)
    pair_real, pair_imag = transform(jnp.stack([mixed, filters]), rows_here)
    mixed_real, filter_real = (pair_real[0], pair_real[1])
    mixed_imag, filter_imag = (pair_imag[0], pair_imag[1])
    conv_real = mixed_real * filter_real - mixed_imag * filter_imag
    conv_imag = mixed_real * filter_imag + mixed_imag * filter_real
    conved = restore(conv_real[None], conv_imag[None], rows_here)[0]
    inner = conved + skip_gain * mixed
    gated = queries * inner
    scale = lax.rsqrt(channel_total(gated * gated) / CHANNELS + eps)[..., None]
    layer_value = gated * scale * norm_gain
    scaled = incoming * norm_gain
    moment = (channel_total(scaled * gated) / CHANNELS)[..., None]
    d_gated = scale * scaled - gated * scale**3 * moment
    d_conv = d_gated * queries
    conv_grad = rounded_copy(d_conv)
    d_query = d_gated * inner
    grad_real, grad_imag = transform(conv_grad[None], rows_here)
    grad_real = grad_real[0]
    grad_imag = grad_imag[0]
    back_real = grad_real * filter_real + grad_imag * filter_imag
    back_imag = grad_imag * filter_real - grad_real * filter_imag
    lag_real = grad_real * mixed_real + grad_imag * mixed_imag
    lag_imag = grad_imag * mixed_real - grad_real * mixed_imag
    back, filter_grad = backward_pair(back_real, back_imag, lag_real, lag_imag, rows_here)
    d_mixed = back + skip_gain * d_conv
    return (layer_value, d_query, d_mixed * value_part, d_mixed * key_part, filter_grad)


def per_device(features, short_filter, long_filter, skip_gain, norm_gain, out_grad):
    tap_count = short_filter.shape[1]
    margin = tap_count - 1
    rows_here = features.shape[1]
    inputs = features.astype(jnp.float32)
    previous = neighbour_rows(inputs[:, rows_here - margin :, :], 1)
    extended = jnp.concatenate([previous, inputs], axis=1)
    branches = jnp.zeros(inputs.shape, jnp.float32)
    for offset in range(tap_count):
        branches = (
            branches
            + short_filter[:, offset, None, :]
            * extended[:, margin - offset : margin - offset + rows_here, :]
        )
    filters = long_filter.astype(jnp.float32)
    incoming = out_grad.astype(jnp.float32)
    results = layer_core(
        branches[0], branches[1], branches[2], filters, incoming, skip_gain, norm_gain, rows_here
    )
    layer_out = results[0].astype(jnp.bfloat16)
    d_branch = jnp.stack([results[1], results[2], results[3]])
    filter_grad = results[4]
    later = neighbour_rows(d_branch[:, :margin, :], -1)
    padded_grads = jnp.concatenate([d_branch, later], axis=1)
    feature_grad = jnp.zeros(inputs.shape, jnp.float32)
    for offset in range(tap_count):
        feature_grad = (
            feature_grad
            + short_filter[:, offset, None, :] * padded_grads[:, offset : offset + rows_here, :]
        )
    return (layer_out, feature_grad, filter_grad)


def solution(mesh):
    return jax.shard_map(
        per_device,
        mesh=mesh,
        in_specs=(
            P(None, "context", "tensor"),
            P(None, None, "tensor"),
            P("context", "tensor"),
            P("tensor"),
            P("tensor"),
            P("context", "tensor"),
        ),
        out_specs=(P("context", "tensor"), P(None, "context", "tensor"), P("context", "tensor")),
        check_vma=False,
    )
```

profile of v0, /device:TPU:24, one launch (start us, length us, event | category | flops | bytes accessed | tf_op | source)
XLA Modules:
  0.0 566.4 jit_solution(2218889745781626375)
XLA Ops:
  0.6 0.7 slice.130
  1.4 3.5 collective-permute-start
  4.9 0.9 fusion.240
  5.7 0.9 bitcast_convert_fusion.1
  6.7 1.1 convert_element_type.92
  8.4 1.2 copy.45
  9.6 18.2 %all-to-all-start = ((f32[2,1,128,512]{3,0,1,2:T(2,128)}), f32[2,1,128,512]{3,0,1,2:T(2,128)S(1)}, u32[]{:S(2)}, u32[]{:S(2)}) async-start(f32[2,1,128,512]{3,0,1,2:T(2,128)} %copy.45), calls=%async_computation | async-start | bytes 1048576 | tf_op jit(solution)/shard_map/all_to_all | solution.py:38
  27.9 32.3 %all-to-all-done = f32[2,1,128,512]{3,0,1,2:T(2,128)S(1)} async-done(((f32[2,1,128,512]{3,0,1,2:T(2,128)}), f32[2,1,128,512]{3,0,1,2:T(2,128)S(1)}, u32[]{:S(2)}, u32[]{:S(2)}) %all-to-all-start) | async-done | bytes 524320 | tf_op jit(solution)/shard_map/all_to_all | solution.py:38
  60.2 1.9 convolution_bitcast_fusion.1
  62.1 1.9 multiply_subtract_fusion
  64.2 2.4 copy.48
  66.6 6.5 %all-to-all-start.1 = ((f32[4,128,2,512]{3,2,0,1:T(2,128)}), f32[4,128,2,512]{3,2,0,1:T(2,128)}, u32[]{:S(2)}, u32[]{:S(2)}) async-start(f32[4,128,2,512]{3,2,0,1:T(2,128)} %copy.48), calls=%async_computation.1 | async-start | bytes 4194304 | tf_op jit(solution)/shard_map/all_to_all | solution.py:42
  73.1 0.7 fusion.131
  73.8 98.3 %all-to-all-done.1 = f32[4,128,2,512]{3,2,0,1:T(2,128)} async-done(((f32[4,128,2,512]{3,2,0,1:T(2,128)}), f32[4,128,2,512]{3,2,0,1:T(2,128)}, u32[]{:S(2)}, u32[]{:S(2)}) %all-to-all-start.1) | async-done | bytes 2097184 | tf_op jit(solution)/shard_map/all_to_all | solution.py:42
  172.2 2.3 copy.49
  174.5 1.8 fusion.236
  176.2 0.5 copy.50
  176.8 0.5 copy.51
  177.3 2.2 fusion.52
  179.5 2.2 fusion.50
  181.7 0.5 copy.52
  182.8 2.5 fusion
  185.3 1.2 fusion.1
  186.7 0.8 fusion.21
  187.6 0.8 fusion.23
  188.4 0.8 fusion.6
  189.2 0.9 subtract_bitcast_fusion.1
  190.2 1.6 copy.56
  191.8 59.7 %all_to_all.99 = f32[2,2,128,512]{3,1,0,2:T(2,128)S(1)} all-to-all(f32[2,2,128,512]{3,1,0,2:T(2,128)} %copy.56), channel_id=1, replica_groups=mesh['tensor'=8,'context'=64] {'context'}, dimensions={2} | all-to-all | bytes 2097152 | tf_op jit(solution)/shard_map/all_to_all | solution.py:38
  253.1 0.6 fusion.72
  253.7 0.6 fusion.9
  254.5 25.4 %all_to_all.100 = f32[1,64,2,512]{3,2,0,1:T(2,128)S(1)} all-to-all(f32[1,64,2,512]{3,2,0,1:T(2,128)S(1)} %copy.60), channel_id=1, replica_groups=mesh['tensor'=8,'context'=64] {'context'}, dimensions={1} | all-to-all | bytes 524288 | tf_op jit(solution)/shard_map/all_to_all | solution.py:42
  280.3 12.4 %all-reduce = (f32[128]{0:T(128)S(1)}, f32[128]{0:T(128)S(1)}) all-reduce(f32[128]{0:T(128)S(1)} %get-tuple-element.4, f32[128]{0:T(128)S(1)} %get-tuple-element.3), channel_id=1, replica_groups=mesh['tensor'=8,'context'=64] {'tensor'}, use_global_device_ids=true, to_apply=%region_1.2 | all-reduce | flops 256 | bytes 2048 | tf_op jit(solution)/shard_map/psum | solution.py:50
  293.2 27.2 %all_to_all.101 = f32[1,1,128,512]{3,1,0,2:T(1,128)S(1)} all-to-all(f32[1,1,128,512]{3,1,0,2:T(1,128)S(1)} %copy.61), channel_id=1, replica_groups=mesh['tensor'=8,'context'=64] {'context'}, dimensions={2} | all-to-all | bytes 524288 | tf_op jit(solution)/shard_map/all_to_all | solution.py:38
  320.4 0.6 reduce
  321.2 1.1 convolution_bitcast_fusion.3
  322.3 1.1 multiply_subtract_fusion.3
  323.5 1.4 copy.64
  324.9 60.7 %all_to_all.102 = f32[2,128,2,512]{3,2,0,1:T(2,128)S(1)} all-to-all(f32[2,128,2,512]{3,2,0,1:T(2,128)} %copy.64), channel_id=1, replica_groups=mesh['tensor'=8,'context'=64] {'context'}, dimensions={1} | all-to-all | bytes 2097152 | tf_op jit(solution)/shard_map/all_to_all | solution.py:42
  386.8 1.6 fusion.39
  388.5 1.6 fusion.43
  390.1 1.1 copy.68
  391.1 1.2 copy.69
  392.4 1.9 fusion.4
  394.3 2.1 multiply_subtract_fusion.2
  396.3 1.2 fusion.10
  397.6 1.2 fusion.11
  398.8 1.2 convolution_add_fusion
  400.1 1.4 subtract_bitcast_fusion
  401.6 2.4 copy.72
  404.1 104.5 %all_to_all.103 = f32[4,2,128,512]{3,1,0,2:T(2,128)S(1)} all-to-all(f32[4,2,128,512]{3,1,0,2:T(2,128)} %copy.72), channel_id=1, replica_groups=mesh['tensor'=8,'context'=64] {'context'}, dimensions={2} | all-to-all | bytes 4194304 | tf_op jit(solution)/shard_map/all_to_all | solution.py:38
  508.6 0.7 copy.73
  509.3 1.8 fusion.235
  511.5 0.7 slice.124
  512.3 1.6 copy.74
  513.8 1.7 slice.122
  515.6 2.1 fusion.65
  517.6 0.9 fusion.3
  519.0 37.0 %all_to_all.104 = f32[2,64,2,512]{3,2,0,1:T(2,128)S(1)} all-to-all(f32[2,64,2,512]{3,2,0,1:T(2,128)S(1)} %copy.76), channel_id=1, replica_groups=mesh['tensor'=8,'context'=64] {'context'}, dimensions={1} | all-to-all | bytes 1048576 | tf_op jit(solution)/shard_map/all_to_all | solution.py:42
  556.3 0.9 multiply_bitcast_fusion.1
  557.3 2.8 collective-permute-start.1
  560.0 0.9 squeeze.26
  560.9 4.0 collective-permute-done.1
  565.0 1.1 fusion.16
  (102 shorter events, 6.9 us)
Async XLA Ops:
  1.4 6.4 %collective-permute-start = (f32[3,2,512]{2,1,0:T(2,128)S(1)}, f32[3,2,512]{2,1,0:T(2,128)S(1)}, u32[]{:S(2)}, u32[]{:S(2)}) collective-permute-start(f32[3,2,512]{2,1,0:T(2,128)S(1)} %slice.130), channel_id=1, source_target_pairs={{0,1},{1,2},{2,3},{3,4},{4,5},{5,6},{6,7},{7,8},{8,9},{9,10},{10,1... | collective-permute-start | bytes 36872 | tf_op jit(solution)/shard_map/ppermute | solution.py:18
  7.8 0.6 copy-start.10
  9.6 50.7 %all-to-all-start = ((f32[2,1,128,512]{3,0,1,2:T(2,128)}), f32[2,1,128,512]{3,0,1,2:T(2,128)S(1)}, u32[]{:S(2)}, u32[]{:S(2)}) async-start(f32[2,1,128,512]{3,0,1,2:T(2,128)} %copy.45), calls=%async_computation | async-start | bytes 1048576 | tf_op jit(solution)/shard_map/all_to_all | solution.py:38
  27.9 36.2 %copy-start.18 = (f32[128,2]{0,1:T(2,128)}, f32[128,2]{0,1:T(2,128)S(1)}, u32[]{:S(2)}) copy-start(f32[128,2]{0,1:T(2,128)S(1)} %get-tuple-element.43) | copy-start | bytes 3076
  27.9 36.2 %copy-start.20 = (f32[128,2]{0,1:T(2,128)}, f32[128,2]{0,1:T(2,128)S(1)}, u32[]{:S(2)}) copy-start(f32[128,2]{0,1:T(2,128)S(1)} %get-tuple-element.44) | copy-start | bytes 3076
  66.6 105.5 %all-to-all-start.1 = ((f32[4,128,2,512]{3,2,0,1:T(2,128)}), f32[4,128,2,512]{3,2,0,1:T(2,128)}, u32[]{:S(2)}, u32[]{:S(2)}) async-start(f32[4,128,2,512]{3,2,0,1:T(2,128)} %copy.48), calls=%async_computation.1 | async-start | bytes 4194304 | tf_op jit(solution)/shard_map/all_to_all | solution.py:42
  177.3 4.4 copy-start.3
  182.8 2.5 copy-start.2
  186.6 1.0 copy-start
  186.7 2.5 copy-start.14
  186.7 2.5 copy-start.16
  253.1 27.0 %copy-start.8 = (bf16[128,512]{1,0:T(8,128)(2,1)S(1)}, bf16[128,512]{1,0:T(8,128)(2,1)}, u32[]{:S(2)}) copy-start(bf16[128,512]{1,0:T(8,128)(2,1)} %param.11) | copy-start | bytes 393220
  253.6 26.4 %copy-start.12 = (f32[512]{0:T(512)S(1)}, f32[512]{0:T(512)}, u32[]{:S(2)}) copy-start(f32[512]{0:T(512)} %param.10) | copy-start | bytes 6148
  253.7 26.4 %copy-start.22 = (f32[512]{0:T(512)S(1)}, f32[512]{0:T(512)}, u32[]{:S(2)}) copy-start(f32[512]{0:T(512)} %param.9) | copy-start | bytes 6148
  280.1 41.2 %copy-start.4 = (f32[128,512]{1,0:T(8,128)}, f32[128,512]{1,0:T(8,128)S(1)}, u32[]{:S(2)}) copy-start(f32[128,512]{1,0:T(8,128)S(1)} %squeeze_squeeze.3) | copy-start | bytes 786436
  280.2 43.1 %copy-start.6 = (f32[128,512]{1,0:T(8,128)}, f32[128,512]{1,0:T(8,128)S(1)}, u32[]{:S(2)}) copy-start(f32[128,512]{1,0:T(8,128)S(1)} %get-tuple-element.9) | copy-start | bytes 786436
  280.3 42.0 %copy-start.19 = (f32[128,2]{0,1:T(2,128)S(1)}, f32[128,2]{0,1:T(2,128)}, u32[]{:S(2)}) copy-start(f32[128,2]{0,1:T(2,128)} %copy-done.18) | copy-start | bytes 3076
  280.3 42.0 %copy-start.21 = (f32[128,2]{0,1:T(2,128)S(1)}, f32[128,2]{0,1:T(2,128)}, u32[]{:S(2)}) copy-start(f32[128,2]{0,1:T(2,128)} %copy-done.20) | copy-start | bytes 3076
  292.7 28.3 %copy-start.24 = (f32[128]{0:T(128)}, f32[128]{0:T(128)S(1)}, u32[]{:S(2)}) copy-start(f32[128]{0:T(128)S(1)} %broadcast_multiply_fusion) | copy-start | bytes 1540
  292.7 28.3 %copy-start.26 = (f32[128]{0:T(128)}, f32[128]{0:T(128)S(1)}, u32[]{:S(2)}) copy-start(f32[128]{0:T(128)S(1)} %get-tuple-element.39) | copy-start | bytes 1540
  292.7 28.3 %copy-start.28 = (f32[128]{0:T(128)}, f32[128]{0:T(128)S(1)}, u32[]{:S(2)}) copy-start(f32[128]{0:T(128)S(1)} %get-tuple-element.40) | copy-start | bytes 1540
  390.1 4.2 copy-start.1
  398.8 1.3 copy-start.15
  398.8 1.3 copy-start.17
  518.5 37.7 %copy-start.5 = (f32[128,512]{1,0:T(8,128)S(1)}, f32[128,512]{1,0:T(8,128)}, u32[]{:S(2)}) copy-start(f32[128,512]{1,0:T(8,128)} %copy-done.4) | copy-start | bytes 786436
  518.5 37.7 %copy-start.7 = (f32[128,512]{1,0:T(8,128)S(1)}, f32[128,512]{1,0:T(8,128)}, u32[]{:S(2)}) copy-start(f32[128,512]{1,0:T(8,128)} %copy-done.6) | copy-start | bytes 786436
  518.9 37.3 %copy-start.9 = (bf16[128,512]{1,0:T(8,128)(2,1)S(1)}, bf16[128,512]{1,0:T(8,128)(2,1)}, u32[]{:S(2)}) copy-start(bf16[128,512]{1,0:T(8,128)(2,1)} %param.11) | copy-start | bytes 393220
  518.9 37.3 %copy-start.13 = (f32[512]{0:T(512)S(1)}, f32[512]{0:T(512)}, u32[]{:S(2)}) copy-start(f32[512]{0:T(512)} %param.10) | copy-start | bytes 6148
  518.9 37.3 %copy-start.23 = (f32[512]{0:T(512)S(1)}, f32[512]{0:T(512)}, u32[]{:S(2)}) copy-start(f32[512]{0:T(512)} %param.9) | copy-start | bytes 6148
  518.9 37.3 %copy-start.25 = (f32[128]{0:T(128)S(1)}, f32[128]{0:T(128)}, u32[]{:S(2)}) copy-start(f32[128]{0:T(128)} %copy-done.24) | copy-start | bytes 1540
  519.0 37.3 %copy-start.27 = (f32[128]{0:T(128)S(1)}, f32[128]{0:T(128)}, u32[]{:S(2)}) copy-start(f32[128]{0:T(128)} %copy-done.26) | copy-start | bytes 1540
  519.0 37.3 %copy-start.29 = (f32[128]{0:T(128)S(1)}, f32[128]{0:T(128)}, u32[]{:S(2)}) copy-start(f32[128]{0:T(128)} %copy-done.28) | copy-start | bytes 1540
  557.2 7.9 %copy-start.11 = (f32[3,1,512]{2,0,1:T(4,128)S(1)}, f32[3,1,512]{2,0,1:T(4,128)}, u32[]{:S(2)}) copy-start(f32[3,1,512]{2,0,1:T(4,128)} %copy-done.10) | copy-start | bytes 18436
  557.3 7.7 %collective-permute-start.1 = (f32[3,2,512]{2,1,0:T(2,128)S(1)}, f32[3,2,512]{2,1,0:T(2,128)S(1)}, u32[]{:S(2)}, u32[]{:S(2)}) collective-permute-start(f32[3,2,512]{2,1,0:T(2,128)S(1)} %slice.149), channel_id=1, source_target_pairs={{1,0},{2,1},{3,2},{4,3},{5,4},{6,5},{7,6},{8,7},{9,8},{10,9},{11,1... | collective-permute-start | bytes 36872 | tf_op jit(solution)/shard_map/ppermute | solution.py:18
where the time goes:
time: 573 us; the launch traced here: 566 us
  blocking collectives  327 us (57%)
  waiting for transfers between devices  135 us (24%)
  matrix products  33.8 us (6%)
  local copies, waits for them, and re-layouts  31.4 us (5%)
  starting transfers between devices  30.9 us (5%)
  other arithmetic  6.78 us (1%)
    all_to_all x3, blocking collectives, to_columns(): lax.all_to_all(blocks, 'context', split_axis=2, concat_axis=1, tiled=True)  191 us
    all_to_all x3, blocking collectives, to_rows(): lax.all_to_all(blocks, 'context', split_axis=1, concat_axis=2, tiled=True)  123 us
    all_to_all x1, waiting for transfers between devices, to_rows(): lax.all_to_all(blocks, 'context', split_axis=1, concat_axis=2, tiled=True)  98.3 us
    dot_general x24, matrix products, contract(): jnp.einsum(pattern, matrix, values, precision=exact_mode, preferred_eleme...  33.8 us
    all_to_all x1, waiting for transfers between devices, to_columns(): lax.all_to_all(blocks, 'context', split_axis=2, concat_axis=1, tiled=True)  32.3 us
    all_to_all x1, starting transfers between devices, to_columns(): lax.all_to_all(blocks, 'context', split_axis=2, concat_axis=1, tiled=True)  18.2 us
    psum x1, blocking collectives, channel_total(): return lax.psum(jnp.sum(values, axis=-1), 'tensor')  12.4 us
  transfers between devices with their start and end apart: 4, of which 3 were waited for; matrix products, arithmetic and copies ran while one was open for 1% of the time, Pallas kernels for 0%

commit v1 on v0

v1 whole, which is shorter than its diff:
```python
import functools

import jax
import jax.numpy as jnp
import numpy as np
from jax import lax
from jax.sharding import PartitionSpec as P

CHANNELS = 4096
EPS = 1e-06


def constants(blocks, width):
    length = 2 * blocks * width
    doubled = 2 * blocks
    a = np.arange(blocks)
    k1 = np.arange(blocks) + 0.5
    first = 2.0 * np.pi * k1[:, None] * a[None, :] / doubled
    f1 = np.concatenate([np.cos(first), -np.sin(first)], axis=0)
    g1 = np.concatenate([np.cos(first.T), -np.sin(first.T)], axis=1) * (2.0 / length)
    b = np.arange(width)
    twist = 2.0 * np.pi * k1[:, None] * b[None, :] / length
    second = 2.0 * np.pi * ((b[:, None] * b[None, :]) % width) / width
    c, s = np.cos(second), np.sin(second)
    f2 = np.block([[c, -s], [s, c]])
    g2 = np.block([[c, s], [-s, c]])
    return [x.astype(np.float32) for x in (f1, f2, g1, g2, np.cos(twist), np.sin(twist))]


def mm(spec, a, b):
    return jnp.einsum(spec, a, b, precision=lax.Precision.HIGHEST, preferred_element_type=jnp.float32)


def forward(x, consts):
    f1, f2, _, _, wr, wi = consts
    blocks = x.shape[1]
    z = mm("ka,sacb->sckb", f1, x)
    re, im = z[:, :, :blocks], z[:, :, blocks:]
    t = jnp.concatenate([re * wr + im * wi, im * wr - re * wi], axis=-1)
    return mm("sckb,bn->sckn", t, f2)


def inverse(spec, consts):
    _, _, g1, g2, wr, wi = consts
    width = spec.shape[-1] // 2
    t = mm("sckn,nb->sckb", spec, g2)
    re, im = t[..., :width], t[..., width:]
    u = jnp.concatenate([re * wr - im * wi, im * wr + re * wi], axis=2)
    return mm("ak,sckb->sacb", g1, u)


def times(p, q, conj):
    w = p.shape[-1] // 2
    pr, pi, qr, qi = p[..., :w], p[..., w:], q[..., :w], q[..., w:]
    if conj:
        qi = -qi
    return jnp.concatenate([pr * qr - pi * qi, pr * qi + pi * qr], axis=-1)


def to_columns(fields):
    n = lax.axis_size("context")
    s, rows, channels = fields.shape
    parts = jnp.swapaxes(fields, 1, 2).reshape(s, n, channels // n, rows)
    return lax.all_to_all(parts, "context", split_axis=1, concat_axis=1, tiled=True)


def to_rows(cols):
    s, n, ch, rows = cols.shape
    back = lax.all_to_all(cols, "context", split_axis=1, concat_axis=1, tiled=True)
    return jnp.swapaxes(back.reshape(s, n * ch, rows), 1, 2)


def rounded_copy(values):
    return lax.optimization_barrier(values.astype(jnp.bfloat16)).astype(jnp.float32)


def channel_total(values):
    return lax.psum(jnp.sum(values, axis=-1), "tensor")


def neighbour_rows(block, by):
    size = lax.axis_size("context")
    pairs = [(i, i + by) for i in range(size) if 0 <= i + by < size]
    return lax.ppermute(block, "context", pairs)


def per_device(features, short_filter, long_filter, skip_gain, norm_gain, out_grad):
    taps = short_filter.shape[1]
    margin = taps - 1
    rows = features.shape[1]
    consts = constants(lax.axis_size("context"), rows)
    inputs = features.astype(jnp.float32)
    previous = neighbour_rows(inputs[:, rows - margin :, :], 1)
    extended = jnp.concatenate([previous, inputs], axis=1)
    branches = sum(
        short_filter[:, j, None, :] * extended[:, margin - j : margin - j + rows, :]
        for j in range(taps)
    )
    queries, key_part, value_part = branches[0], branches[1], branches[2]
    filters = long_filter.astype(jnp.float32)
    incoming = out_grad.astype(jnp.float32)
    mixed = rounded_copy(key_part * value_part)
    specs = forward(to_columns(jnp.stack([mixed, filters])), consts)
    mixed_s, filter_s = specs[0:1], specs[1:2]
    conved = to_rows(inverse(times(mixed_s, filter_s, False), consts))[0]
    inner = conved + skip_gain * mixed
    gated = queries * inner
    scaled = incoming * norm_gain
    sums = lax.psum(
        jnp.stack([jnp.sum(gated * gated, axis=-1), jnp.sum(scaled * gated, axis=-1)]), "tensor"
    )
    scale = lax.rsqrt(sums[0] / CHANNELS + EPS)[:, None]
    moment = (sums[1] / CHANNELS)[:, None]
    layer_out = (gated * scale * norm_gain).astype(jnp.bfloat16)
    d_gated = scale * scaled - gated * scale**3 * moment
    d_conv = d_gated * queries
    d_query = d_gated * inner
    grad_s = forward(to_columns(rounded_copy(d_conv)[None]), consts)
    pair = to_rows(
        inverse(jnp.concatenate([times(grad_s, filter_s, True), times(grad_s, mixed_s, True)]), consts)
    )
    back, filter_grad = pair[0], pair[1]
    d_mixed = back + skip_gain * d_conv
    d_branch = jnp.stack([d_query, d_mixed * value_part, d_mixed * key_part])
    later = neighbour_rows(d_branch[:, :margin, :], -1)
    padded = jnp.concatenate([d_branch, later], axis=1)
    feature_grad = sum(
        short_filter[:, j, None, :] * padded[:, j : j + rows, :] for j in range(taps)
    )
    return (layer_out, feature_grad, filter_grad)


def solution(mesh):
    return jax.shard_map(
        per_device,
        mesh=mesh,
        in_specs=(
            P(None, "context", "tensor"),
            P(None, None, "tensor"),
            P("context", "tensor"),
            P("tensor"),
            P("tensor"),
            P("context", "tensor"),
        ),
        out_specs=(P("context", "tensor"), P(None, "context", "tensor"), P("context", "tensor")),
        check_vma=False,
    )
```

time: 573 us -> 186 us (0.32)
  blocking collectives: 327 us -> 127 us
  waiting for transfers between devices: 135 us -> 25.7 us
  matrix products: 33.8 us -> 6.01 us
  local copies, waits for them, and re-layouts: 31.4 us -> 8.29 us
  starting transfers between devices: 30.9 us -> 12.2 us
    all_to_all x6 -> x3, blocking collectives: 315 us -> 115 us  [the longest x2 77.9 us: to_columns(): lax.all_to_all(parts, 'context', split_axis=1, concat_axis=1, tiled=True)]
    all_to_all x2 -> x1, waiting for transfers between devices: 131 us -> 20.6 us  [to_rows(): lax.all_to_all(cols, 'context', split_axis=1, concat_axis=1, tiled=True)]
    dot_general x24 -> x8, matrix products: 33.8 us -> 6.01 us  [mm(): jnp.einsum(spec, a, b, precision=lax.Precision.HIGHEST, preferred_element...]
    all_to_all x2 -> x1, starting transfers between devices: 24.7 us -> 5.93 us  [to_rows(): lax.all_to_all(cols, 'context', split_axis=1, concat_axis=1, tiled=True)]
    slice x19 -> x3, local copies, waits for them, and re-layouts: 13.8 us -> 0.45 us  [the longest x2 0.43 us: per_device(): previous = neighbour_rows(inputs[:, rows - margin:, :], 1)]
    concatenate x4 -> x0, local copies, waits for them, and re-layouts: 7.79 us -> none  [the longest x2 4.03 us: restore(): arrived = to_columns(jnp.concatenate([twist_real, twist_imag], axis=0))]
  transfers between devices with their start and end apart: 4 -> 3, of which waited for: 3 -> 3; matrix products, arithmetic and copies ran while one was open for 1% -> 1% of each run, Pallas kernels for 0% -> 0%
where the time goes in v1:
time: 186 us; the launch traced here: 185 us
  blocking collectives  127 us (68%)
  waiting for transfers between devices  25.7 us (14%)
  starting transfers between devices  12.2 us (7%)
  local copies, waits for them, and re-layouts  8.29 us (4%)
  matrix products  6.01 us (3%)
  other arithmetic  4.21 us (2%)
    all_to_all x2, blocking collectives, to_columns(): lax.all_to_all(parts, 'context', split_axis=1, concat_axis=1, tiled=True)  77.9 us
    all_to_all x1, blocking collectives, to_rows(): lax.all_to_all(cols, 'context', split_axis=1, concat_axis=1, tiled=True)  36.8 us
    all_to_all x1, waiting for transfers between devices, to_rows(): lax.all_to_all(cols, 'context', split_axis=1, concat_axis=1, tiled=True)  20.6 us
    psum x1, blocking collectives, per_device(): lax.psum(jnp.stack([jnp.sum(gated * gated, axis=-1), jnp.sum(scaled * gat...  12.4 us
    ppermute x2, starting transfers between devices, neighbour_rows(): return lax.ppermute(block, 'context', pairs)  6.25 us
    dot_general x8, matrix products, mm(): jnp.einsum(spec, a, b, precision=lax.Precision.HIGHEST, preferred_element...  6.01 us
    all_to_all x1, starting transfers between devices, to_rows(): lax.all_to_all(cols, 'context', split_axis=1, concat_axis=1, tiled=True)  5.93 us
    unnamed x38, local copies, waits for them, and re-layouts  5.75 us
  transfers between devices with their start and end apart: 3, of which 3 were waited for; matrix products, arithmetic and copies ran while one was open for 1% of the time, Pallas kernels for 0%

profile of v1, /device:TPU:24, one launch (start us, length us, event | category | flops | bytes accessed | tf_op | source)
XLA Modules:
  0.0 184.7 jit_solution(1027472803582006508)
XLA Ops:
  0.6 0.0 copy-start.13
  0.7 1.2 copy.29
  1.9 0.2 slice.135
  2.1 0.3 copy.30
  2.3 3.5 %collective-permute-start = (f32[3,2,512]{2,1,0:T(2,128)S(1)}, f32[3,2,512]{2,1,0:T(2,128)S(1)}, u32[]{:S(2)}, u32[]{:S(2)}) collective-permute-start(f32[3,2,512]{2,1,0:T(2,128)S(1)} %copy.30), channel_id=1, source_target_pairs={{0,1},{1,2},{2,3},{3,4},{4,5},{5,6},{6,7},{7,8},{8,9},{9,10},{10,1... | collective-permute-start | bytes 36872 | tf_op jit(solution)/shard_map/ppermute | solution.py:84
  5.9 0.1 copy.32
  6.1 0.1 convert_element_type.20
  6.1 1.8 collective-permute-done
  7.9 0.3 copy.31
  8.2 1.4 fusion.18
  9.7 0.0 copy-start.11
  9.8 0.0 copy-start
  9.8 0.0 copy-start.1
  9.8 50.6 %all_to_all.20 = f32[2,64,8,128]{3,2,0,1:T(8,128)S(1)} all-to-all(f32[2,64,8,128]{3,2,0,1:T(8,128)S(1)} %copy.33), channel_id=1, replica_groups=mesh['tensor'=8,'context'=64] {'context'}, dimensions={1} | all-to-all | bytes 1048576 | tf_op jit(solution)/shard_map/all_to_all | solution.py:64
  60.4 0.0 copy-done.11
  60.4 1.1 convolution_bitcast_fusion
  61.5 0.1 multiply_add_fusion.1
  61.7 0.0 copy-start.4
  61.7 1.0 fusion
  62.7 0.1 multiply_subtract_fusion.7
  62.8 0.0 copy-start.10
  62.8 0.0 copy-done.4
  62.8 0.6 convolution_bitcast_fusion.3
  63.4 0.0 copy-start.7
  63.4 0.0 copy-start.12
  63.4 0.0 copy-start.14
  63.4 0.1 multiply_subtract_fusion.6
  63.5 0.0 copy-done.10
  63.6 0.4 convolution_bitcast_fusion.5
  64.0 0.9 copy.35
  64.8 5.9 %all-to-all-start.1 = ((f32[1,64,8,128]{3,2,0,1:T(8,128)}), f32[1,64,8,128]{3,2,0,1:T(8,128)S(1)}, u32[]{:S(2)}, u32[]{:S(2)}) async-start(f32[1,64,8,128]{3,2,0,1:T(8,128)} %copy.35), calls=%async_computation.1 | async-start | bytes 524288 | tf_op jit(solution)/shard_map/all_to_all | solution.py:69
  70.8 0.0 copy-done.7
  70.8 0.0 copy-start.9
  70.8 0.1 copy.36
  70.9 20.6 %all-to-all-done.1 = f32[1,64,8,128]{3,2,0,1:T(8,128)S(1)} async-done(((f32[1,64,8,128]{3,2,0,1:T(8,128)}), f32[1,64,8,128]{3,2,0,1:T(8,128)S(1)}, u32[]{:S(2)}, u32[]{:S(2)}) %all-to-all-start.1) | async-done | bytes 262176 | tf_op jit(solution)/shard_map/all_to_all | solution.py:69
  91.5 0.2 multiply_reduce_fusion.1
  91.7 12.4 %psum.7 = f32[2,128]{1,0:T(2,128)S(1)} all-reduce(f32[2,128]{1,0:T(2,128)S(1)} %pad_maximum_fusion.3), channel_id=1, replica_groups=mesh['tensor'=8,'context'=64] {'tensor'}, use_global_device_ids=true, to_apply=%region_2.0 | all-reduce | flops 256 | bytes 2048 | tf_op jit(solution)/shard_map/psum | solution.py:109
  104.2 0.1 fusion.35
  104.3 0.0 copy-start.3
  104.4 27.4 %all_to_all.21 = f32[1,64,8,128]{3,2,0,1:T(8,128)S(1)} all-to-all(f32[1,64,8,128]{3,2,0,1:T(8,128)S(1)} %convert_bitcast_fusion.1), channel_id=1, replica_groups=mesh['tensor'=8,'context'=64] {'context'}, dimensions={1} | all-to-all | bytes 524288 | tf_op jit(solution)/shard_map/all_to_all | solution.py:64
  131.8 0.6 convolution_bitcast_fusion.2
  132.4 0.1 multiply_add_fusion.4
  132.5 0.6 convolution_bitcast_fusion.1
  133.1 0.0 copy-start.2
  133.1 0.2 multiply_subtract_fusion.3
  133.2 0.8 copy-done.2
  134.0 1.0 fusion.4
  135.0 0.0 copy-start.8
  135.0 0.1 multiply_subtract_fusion
  135.2 0.6 copy-done.8
  135.8 0.7 convolution_bitcast_fusion.4
  136.5 0.3 copy.39
  136.8 36.8 %all_to_all.22 = f32[2,64,8,128]{3,2,0,1:T(8,128)S(1)} all-to-all(f32[2,64,8,128]{3,2,0,1:T(8,128)S(1)} %copy.39), channel_id=1, replica_groups=mesh['tensor'=8,'context'=64] {'context'}, dimensions={1} | all-to-all | bytes 1048576 | tf_op jit(solution)/shard_map/all_to_all | solution.py:69
  173.7 0.2 multiply_bitcast_fusion.1
  173.9 0.1 pad_maximum_fusion.2
  174.0 0.3 copy.41
  174.3 2.8 %collective-permute-start.1 = (f32[3,2,512]{2,1,0:T(2,128)S(1)}, f32[3,2,512]{2,1,0:T(2,128)S(1)}, u32[]{:S(2)}, u32[]{:S(2)}) collective-permute-start(f32[3,2,512]{2,1,0:T(2,128)S(1)} %copy.41), channel_id=1, source_target_pairs={{1,0},{2,1},{3,2},{4,3},{5,4},{6,5},{7,6},{8,7},{9,8},{10,9},{11,1... | collective-permute-start | bytes 36872 | tf_op jit(solution)/shard_map/ppermute | solution.py:84
  177.1 0.8 copy.45
  177.9 0.8 copy.43
  178.7 3.3 %collective-permute-done.1 = f32[3,2,512]{2,1,0:T(2,128)S(1)} collective-permute-done((f32[3,2,512]{2,1,0:T(2,128)S(1)}, f32[3,2,512]{2,1,0:T(2,128)S(1)}, u32[]{:S(2)}, u32[]{:S(2)}) %collective-permute-start.1) | collective-permute-done | bytes 12320 | tf_op jit(solution)/shard_map/ppermute | solution.py:84
  182.0 0.3 copy.42
  182.3 0.1 pad_maximum_fusion
  182.4 1.2 fusion.19
  183.6 1.1 copy.44
  (26 shorter events, 0.3 us)
Async XLA Ops:
  0.6 5.2 %copy-start.13 = (f32[3,3,512]{2,1,0:T(4,128)S(1)}, f32[3,3,512]{2,1,0:T(4,128)}, u32[]{:S(2)}) copy-start(f32[3,3,512]{2,1,0:T(4,128)} %param.17) | copy-start | bytes 55300
  0.6 5.2 %copy-start.6 = (bf16[128,512]{1,0:T(8,128)(2,1)S(1)}, bf16[128,512]{1,0:T(8,128)(2,1)}, u32[]{:S(2)}) copy-start(bf16[128,512]{1,0:T(8,128)(2,1)} %param.18) | copy-start | bytes 393220
  2.3 5.6 %collective-permute-start = (f32[3,2,512]{2,1,0:T(2,128)S(1)}, f32[3,2,512]{2,1,0:T(2,128)S(1)}, u32[]{:S(2)}, u32[]{:S(2)}) collective-permute-start(f32[3,2,512]{2,1,0:T(2,128)S(1)} %copy.30), channel_id=1, source_target_pairs={{0,1},{1,2},{2,3},{3,4},{4,5},{5,6},{6,7},{7,8},{8,9},{9,10},{10,1... | collective-permute-start | bytes 36872 | tf_op jit(solution)/shard_map/ppermute | solution.py:84
  9.7 50.7 %copy-start.11 = (f32[128,64,1,1]{0,1,3,2:T(8,128)S(1)}, f32[128,64,1,1]{0,1,3,2:T(8,128)}, u32[]{:S(2)}) copy-start(f32[128,64,1,1]{0,1,3,2:T(8,128)} %constant.26) | copy-start | bytes 98308
  9.8 51.7 %copy-start = (f32[64,128]{1,0:T(8,128)S(1)}, f32[64,128]{1,0:T(8,128)}, u32[]{:S(2)}) copy-start(f32[64,128]{1,0:T(8,128)} %constant.22.clone) | copy-start | bytes 98308
  9.8 51.7 %copy-start.1 = (f32[64,128]{1,0:T(8,128)S(1)}, f32[64,128]{1,0:T(8,128)}, u32[]{:S(2)}) copy-start(f32[64,128]{1,0:T(8,128)} %constant.21.clone) | copy-start | bytes 98308
  60.4 1.3 copy-start.5
  61.7 1.1 copy-start.4
  62.8 0.8 copy-start.10
  63.4 7.4 %copy-start.7 = (bf16[128,512]{1,0:T(8,128)(2,1)S(1)}, bf16[128,512]{1,0:T(8,128)(2,1)}, u32[]{:S(2)}) copy-start(bf16[128,512]{1,0:T(8,128)(2,1)} %param.21) | copy-start | bytes 393220
  63.4 28.1 %copy-start.12 = (f32[512]{0:T(512)S(1)}, f32[512]{0:T(512)}, u32[]{:S(2)}) copy-start(f32[512]{0:T(512)} %param.20) | copy-start | bytes 6148
  63.4 28.1 %copy-start.14 = (f32[512]{0:T(512)S(1)}, f32[512]{0:T(512)}, u32[]{:S(2)}) copy-start(f32[512]{0:T(512)} %param.19) | copy-start | bytes 6148
  64.8 26.7 %all-to-all-start.1 = ((f32[1,64,8,128]{3,2,0,1:T(8,128)}), f32[1,64,8,128]{3,2,0,1:T(8,128)S(1)}, u32[]{:S(2)}, u32[]{:S(2)}) async-start(f32[1,64,8,128]{3,2,0,1:T(8,128)} %copy.35), calls=%async_computation.1 | async-start | bytes 524288 | tf_op jit(solution)/shard_map/all_to_all | solution.py:69
  70.8 61.0 %copy-start.9 = (f32[128,64,1]{0,1,2:T(8,128)S(1)}, f32[128,64,1]{0,1,2:T(8,128)}, u32[]{:S(2)}) copy-start(f32[128,64,1]{0,1,2:T(8,128)} %constant.30) | copy-start | bytes 98308
  104.3 28.1 %copy-start.3 = (f32[256,256,1]{1,0,2:T(8,128)S(1)}, f32[256,256,1]{1,0,2:T(8,128)}, u32[]{:S(2)}) copy-start(f32[256,256,1]{1,0,2:T(8,128)} %constant.31) | copy-start | bytes 786436
  133.1 1.0 copy-start.2
  135.0 0.8 copy-start.8
  174.3 7.7 %collective-permute-start.1 = (f32[3,2,512]{2,1,0:T(2,128)S(1)}, f32[3,2,512]{2,1,0:T(2,128)S(1)}, u32[]{:S(2)}, u32[]{:S(2)}) collective-permute-start(f32[3,2,512]{2,1,0:T(2,128)S(1)} %copy.41), channel_id=1, source_target_pairs={{1,0},{2,1},{3,2},{4,3},{5,4},{6,5},{7,6},{8,7},{9,8},{10,9},{11,1... | collective-permute-start | bytes 36872 | tf_op jit(solution)/shard_map/ppermute | solution.py:84

commit v2 on v1

v2 whole, which is shorter than its diff:
```python
import functools

import jax
import jax.numpy as jnp
import ml_dtypes
import numpy as np
from jax import lax
from jax.experimental import pallas as pl
from jax.experimental.pallas import tpu as pltpu
from jax.sharding import PartitionSpec as P

CHANNELS = 4096
EPS = 1e-06
F32 = jnp.float32
BF16 = jnp.bfloat16
MESH = pl.DeviceIdType.MESH
RING = 16
SIDE = 4
LANES = 128
CH = 8


def constants(blocks, width):
    length = 2 * blocks * width
    a = np.arange(blocks)
    k1 = np.arange(blocks) + 0.5
    first = 2.0 * np.pi * k1[:, None] * a[None, :] / (2 * blocks)
    f1 = np.concatenate([np.cos(first), -np.sin(first)], axis=0)
    g1 = np.concatenate([np.cos(first.T), -np.sin(first.T)], axis=1) * (2.0 / length)
    b = np.arange(width)
    twist = 2.0 * np.pi * k1[:, None] * b[None, :] / length
    second = 2.0 * np.pi * ((b[:, None] * b[None, :]) % width) / width
    c, s = np.cos(second), np.sin(second)
    f2 = np.block([[c, -s], [s, c]])
    g2 = np.block([[c, s], [-s, c]])

    def split(m):
        high = m.astype(ml_dtypes.bfloat16)
        low = (m - high.astype(np.float64)).astype(ml_dtypes.bfloat16)
        return high, low

    f1h, f1l = split(f1)
    f2h, f2l = split(f2)
    g1h, g1l = split(g1)
    g2h, g2l = split(g2)
    twists = [np.cos(twist).astype(np.float32), np.sin(twist).astype(np.float32)]
    return [np.concatenate([f1h, f1l], axis=0), f2h, f2l, g1h, g1l, g2h, g2l] + twists


def dot(a, b):
    return jnp.dot(a, b, preferred_element_type=F32)


def halves(x):
    high = x.astype(BF16)
    return high, (x - high.astype(F32)).astype(BF16)


def kernel(
    feat, taps, filt, skip, gain, grad,
    f1, f2h, f2l, g1h, g1l, g2h, g2l, wr, wi,
    out, fgrad, hgrad,
    send, recv, qt, kt, vt, mt, st, it, gt, ct, spec_h, spec_x, spec_g, th, tl, db,
    halo_s, halo_r, norm_s, norm_r,
    send_sem, recv_sem, halo_send, halo_recv, norm_send, norm_recv,
):
    me = lax.axis_index("context")
    lane = lax.axis_index("tensor")
    n_ctx = lax.axis_size("context")
    n_ten = lax.axis_size("tensor")
    my_z, my_y = me // SIDE, me % SIDE
    wide = LANES * SIDE
    chunks = [slice(j * LANES, (j + 1) * LANES) for j in range(wide // LANES)]

    def peer(i):
        k = i // SIDE
        odd = k % 2
        dz = odd * ((k + 1) // 2) + (1 - odd) * (RING - k // 2)
        return ((my_z + dz) % RING) * SIDE + (my_y + i % SIDE) % SIDE

    barrier = pltpu.get_barrier_semaphore()

    def greet(i, carry):
        pl.semaphore_signal(barrier, inc=1, device_id={"context": peer(i)}, device_id_type=MESH)
        return carry

    def greet_tensor(i, carry):
        pl.semaphore_signal(
            barrier, inc=1, device_id={"tensor": (lane + i) % n_ten}, device_id_type=MESH
        )
        return carry

    lax.fori_loop(1, n_ctx, greet, 0)
    lax.fori_loop(1, n_ten, greet_tensor, 0)

    def tile(i):
        return pl.ds(pl.multiple_of(i * CH, CH), CH)

    def scatter(u):
        pltpu.make_async_copy(send.at[u, tile(me)], recv.at[u, tile(me)], recv_sem.at[u]).start()

        def body(i, carry):
            p = peer(i)
            pltpu.make_async_remote_copy(
                src_ref=send.at[u, tile(p)],
                dst_ref=recv.at[u, tile(me)],
                send_sem=send_sem.at[u],
                recv_sem=recv_sem.at[u],
                device_id={"context": p},
                device_id_type=MESH,
            ).start()
            return carry

        lax.fori_loop(1, n_ctx, body, 0)

    def arrived(u):
        pltpu.make_async_copy(send.at[u], recv.at[u], recv_sem.at[u]).wait()

    def halo_copy(h, to):
        return pltpu.make_async_remote_copy(
            src_ref=halo_s.at[h],
            dst_ref=halo_r.at[h],
            send_sem=halo_send.at[h],
            recv_sem=halo_recv.at[h],
            device_id={"context": to},
            device_id_type=MESH,
        )

    for j, c in enumerate(chunks):
        send[0, c, :] = filt[:, c].astype(F32).T
    for i in range(3):
        halo_s[0, 2 * i : 2 * i + 2, :] = feat[i, 112:128, :].astype(F32)[14:16]
    halo_s[0, 6:8, :] = jnp.zeros((2, wide), F32)
    pl.semaphore_wait(barrier, n_ctx - 1 + n_ten - 1)

    first_halo = halo_copy(0, (me + 1) % n_ctx)
    first_halo.start()
    scatter(0)

    for j, c in enumerate(chunks):
        st[c, :] = (grad[:, c].astype(F32) * gain[0:1, c]).T
        gt[c, :] = jnp.broadcast_to(skip[0:1, c], (LANES, LANES)).T

    row = lax.broadcasted_iota(jnp.int32, (LANES, LANES), 0)
    first_halo.wait_recv()
    keep = (me > 0).astype(F32)
    for j, c in enumerate(chunks):
        parts = []
        for i in range(3):
            x = feat[i, :, c].astype(F32)
            far = halo_r[0, 2 * i : 2 * i + 1, c] * keep
            near = halo_r[0, 2 * i + 1 : 2 * i + 2, c] * keep
            x1 = jnp.where(row == 0, near, pltpu.roll(x, 1, 0))
            x2 = jnp.where(row == 0, far, jnp.where(row == 1, near, pltpu.roll(x, 2, 0)))
            parts.append(
                taps[3 * i : 3 * i + 1, c] * x
                + taps[3 * i + 1 : 3 * i + 2, c] * x1
                + taps[3 * i + 2 : 3 * i + 3, c] * x2
            )
        qt[c, :] = parts[0].T
        k, v = parts[1].T, parts[2].T
        kt[c, :] = k
        vt[c, :] = v
        send[1, c, :] = (k * v).astype(BF16).astype(F32)
    scatter(1)
    for j, c in enumerate(chunks):
        mt[c, :] = send[1, c, :]

    blocks = 64

    def forward(u, spec):
        for p in range(CH // 2):
            x = jnp.concatenate(
                [recv[u, pl.ds(2 * p + e, blocks, stride=CH), :] for e in range(2)], axis=1
            ).astype(BF16)
            z = dot(f1[...], x)
            z = z[: 2 * blocks] + z[2 * blocks :]
            for e in range(2):
                re = z[:blocks, e * LANES : (e + 1) * LANES]
                im = z[blocks:, e * LANES : (e + 1) * LANES]
                rows = slice((2 * p + e) * blocks, (2 * p + e + 1) * blocks)
                h, l = halves(re * wr[...] + im * wi[...])
                th[rows, :LANES] = h
                tl[rows, :LANES] = l
                h, l = halves(im * wr[...] - re * wi[...])
                th[rows, LANES:] = h
                tl[rows, LANES:] = l
        spec[...] = dot(th[...], f2h[...]) + dot(tl[...], f2h[...]) + dot(th[...], f2l[...])

    def inverse(a, b, sign, u):
        for p in range(CH // 2):
            rows = slice(2 * p * blocks, 2 * (p + 1) * blocks)
            ar, ai = a[rows, :LANES], a[rows, LANES:]
            br, bi = b[rows, :LANES], sign * b[rows, LANES:]
            h, l = halves(ar * br - ai * bi)
            th[rows, :LANES] = h
            tl[rows, :LANES] = l
            h, l = halves(ar * bi + ai * br)
            th[rows, LANES:] = h
            tl[rows, LANES:] = l
        t = dot(th[...], g2h[...]) + dot(tl[...], g2h[...]) + dot(th[...], g2l[...])
        for p in range(CH // 2):
            both = []
            for e in range(2):
                rows = slice((2 * p + e) * blocks, (2 * p + e + 1) * blocks)
                re, im = t[rows, :LANES], t[rows, LANES:]
                both.append(
                    jnp.concatenate(
                        [re * wr[...] - im * wi[...], im * wr[...] + re * wi[...]], axis=0
                    )
                )
            h, l = halves(jnp.concatenate(both, axis=1))
            y = dot(g1h[...], h) + dot(g1h[...], l) + dot(g1l[...], h)
            for e in range(2):
                send[u, pl.ds(2 * p + e, blocks, stride=CH), :] = y[:, e * LANES : (e + 1) * LANES]

    arrived(0)
    forward(0, spec_h)
    arrived(1)
    forward(1, spec_x)
    inverse(spec_x, spec_h, 1.0, 2)
    scatter(2)

    arrived(2)
    square = jnp.zeros((1, LANES), F32)
    cross = jnp.zeros((1, LANES), F32)
    for c in chunks:
        inner = recv[2, c, :] + gt[c, :] * mt[c, :]
        gated = qt[c, :] * inner
        it[c, :] = inner
        ct[c, :] = gated
        square = square + jnp.sum(gated * gated, axis=0, keepdims=True)
        cross = cross + jnp.sum(st[c, :] * gated, axis=0, keepdims=True)
    norm_s[...] = jnp.zeros((8, LANES), F32)
    norm_s[0:1, :] = square
    norm_s[1:2, :] = cross
    pltpu.make_async_copy(norm_s, norm_r.at[lane], norm_recv).start()

    def share(i, carry):
        pltpu.make_async_remote_copy(
            src_ref=norm_s,
            dst_ref=norm_r.at[lane],
            send_sem=norm_send,
            recv_sem=norm_recv,
            device_id={"tensor": (lane + i) % n_ten},
            device_id_type=MESH,
        ).start()
        return carry

    lax.fori_loop(1, n_ten, share, 0)
    pltpu.make_async_copy(norm_r, norm_r, norm_recv).wait()
    total = norm_r[0]
    for i in range(1, 8):
        total = total + norm_r[i]
    scale = lax.rsqrt(total[0:1] / CHANNELS + EPS)
    pull = scale * scale * scale * (total[1:2] / CHANNELS)
    for c in chunks:
        d_gated = scale * st[c, :] - ct[c, :] * pull
        d_conv = d_gated * qt[c, :]
        send[3, c, :] = d_conv.astype(BF16).astype(F32)
        gt[c, :] = gt[c, :] * d_conv
        it[c, :] = d_gated * it[c, :]
    scatter(3)
    for c in chunks:
        out[:, c] = ((ct[c, :] * scale).T * gain[0:1, c]).astype(BF16)
        db[0, :, c] = it[c, :].T

    arrived(3)
    forward(3, spec_g)
    inverse(spec_g, spec_h, -1.0, 4)
    scatter(4)
    inverse(spec_g, spec_x, -1.0, 5)
    scatter(5)

    arrived(4)
    for c in chunks:
        d_mixed = recv[4, c, :] + gt[c, :]
        db[1, :, c] = (d_mixed * vt[c, :]).T
        db[2, :, c] = (d_mixed * kt[c, :]).T
    for i in range(3):
        halo_s[1, 2 * i : 2 * i + 2, :] = db[i, 0:2, :]
    halo_s[1, 6:8, :] = jnp.zeros((2, wide), F32)
    last_halo = halo_copy(1, (me + n_ctx - 1) % n_ctx)
    last_halo.start()
    last_halo.wait_recv()
    keep = (me < n_ctx - 1).astype(F32)
    for c in chunks:
        for i in range(3):
            x = db[i, :, c]
            near = halo_r[1, 2 * i : 2 * i + 1, c] * keep
            far = halo_r[1, 2 * i + 1 : 2 * i + 2, c] * keep
            x1 = jnp.where(row == LANES - 1, near, pltpu.roll(x, LANES - 1, 0))
            x2 = jnp.where(
                row == LANES - 1,
                far,
                jnp.where(row == LANES - 2, near, pltpu.roll(x, LANES - 2, 0)),
            )
            fgrad[i, :, c] = (
                taps[3 * i : 3 * i + 1, c] * x
                + taps[3 * i + 1 : 3 * i + 2, c] * x1
                + taps[3 * i + 2 : 3 * i + 3, c] * x2
            )
    arrived(5)
    for c in chunks:
        hgrad[:, c] = recv[5, c, :].T

    for u in range(6):
        gone = pl.ds(0, (n_ctx - 1) * CH)
        pltpu.make_async_copy(send.at[u, gone], send.at[u, gone], send_sem.at[u]).wait()
    first_halo.wait_send()
    last_halo.wait_send()
    spent = pl.ds(0, n_ten - 1)
    pltpu.make_async_copy(norm_r.at[spent], norm_r.at[spent], norm_send).wait()


def per_device(features, short_filter, long_filter, skip_gain, norm_gain, out_grad):
    rows, wide = long_filter.shape
    vmem = pl.BlockSpec(memory_space=pltpu.VMEM)
    column = pltpu.VMEM((wide, rows), F32)
    spec = pltpu.VMEM((wide, 2 * rows), F32)
    half = pltpu.VMEM((wide, 2 * rows), BF16)
    consts = [jnp.asarray(x) for x in constants(64, rows)]
    out, fgrad, hgrad = pl.pallas_call(
        kernel,
        out_shape=(
            jax.ShapeDtypeStruct((rows, wide), BF16),
            jax.ShapeDtypeStruct((3, rows, wide), F32),
            jax.ShapeDtypeStruct((rows, wide), F32),
        ),
        in_specs=[vmem] * (6 + len(consts)),
        out_specs=[vmem] * 3,
        scratch_shapes=[
            pltpu.VMEM((6, wide, rows), F32),
            pltpu.VMEM((6, wide, rows), F32),
        ]
        + [column] * 8
        + [spec] * 3
        + [half] * 2
        + [
            pltpu.VMEM((3, rows, wide), F32),
            pltpu.VMEM((2, 8, wide), F32),
            pltpu.VMEM((2, 8, wide), F32),
            pltpu.VMEM((8, rows), F32),
            pltpu.VMEM((8, 8, rows), F32),
            pltpu.SemaphoreType.DMA((6,)),
            pltpu.SemaphoreType.DMA((6,)),
            pltpu.SemaphoreType.DMA((2,)),
            pltpu.SemaphoreType.DMA((2,)),
            pltpu.SemaphoreType.DMA,
            pltpu.SemaphoreType.DMA,
        ],
        compiler_params=pltpu.CompilerParams(
            collective_id=0, has_side_effects=True, vmem_limit_bytes=48 * 1024 * 1024
        ),
    )(
        features,
        short_filter.reshape(9, wide),
        long_filter,
        skip_gain.reshape(1, wide),
        norm_gain.reshape(1, wide),
        out_grad,
        *consts,
    )
    return out, fgrad, hgrad


def solution(mesh):
    return jax.shard_map(
        per_device,
        mesh=mesh,
        in_specs=(
            P(None, "context", "tensor"),
            P(None, None, "tensor"),
            P("context", "tensor"),
            P("tensor"),
            P("tensor"),
            P("context", "tensor"),
        ),
        out_specs=(P("context", "tensor"), P(None, "context", "tensor"), P("context", "tensor")),
        check_vma=False,
    )
```

time: 186 us -> 134 us (0.72)
  the two profiles are of different devices: /device:TPU:24 before, /device:TPU:32 now
where the time goes in v2:
time: 134 us; the launch traced here: 133 us
  Pallas kernels  120 us (90%)
  local copies, waits for them, and re-layouts  13.1 us (10%)
    pallas_call x1, Pallas kernels, per_device(): pl.pallas_call(kernel, out_shape=(jax.ShapeDtypeStruct((rows, wide), BF16...  120 us
    unnamed x31, local copies, waits for them, and re-layouts  12.3 us

profile of v2, /device:TPU:32, one launch (start us, length us, event | category | flops | bytes accessed | tf_op | source)
XLA Modules:
  0.0 133.4 jit_solution(11049412031785766010)
XLA Ops:
  0.6 0.0 copy-start.9
  0.6 0.0 copy-start.8
  0.7 0.8 reshape.15.taps
  1.4 0.0 copy-done.9
  1.4 0.0 copy-done.8
  1.4 0.0 copy-start
  1.4 1.0 copy-done
  2.4 0.0 copy-start.1
  2.4 0.9 copy-done.1
  3.3 0.0 copy-start.2
  3.3 0.9 copy-done.2
  4.2 0.0 copy-start.3
  4.2 0.9 copy-done.3
  5.1 0.0 copy-start.4
  5.2 0.9 copy-done.4
  6.1 0.0 copy-start.5
  6.1 0.9 copy-done.5
  7.0 0.0 copy-start.6
  7.0 0.9 copy-done.6
  7.9 0.0 copy-start.7
  7.9 0.8 copy-done.7
  8.7 0.0 copy-start.10
  8.7 0.7 copy-done.10
  9.4 0.0 copy-start.11
  9.4 0.7 copy-done.11
  10.1 0.0 copy-start.12
  10.1 0.7 copy-done.12
  10.8 0.0 copy-start.13
  10.8 0.7 copy-done.13
  11.5 119.7 %shard_map.166 = (bf16[128,512]{1,0:T(8,128)(2,1)S(1)}, f32[3,128,512]{2,1,0:T(8,128)S(1)}, f32[128,512]{1,0:T(8,128)S(1)}) custom-call(bf16[3,128,512]{2,1,0:T(8,128)(2,1)S(1)} %copy-done, f32[9,512]{1,0:T(8,128)S(1)} %reshape.15.taps, bf16[128,512]{1,0:T(8,128)(2,1)S(1)} %copy-done.1, f32[1,512]{1,0:T(1,128)S(1)} %bitcast.2, f32[1,512]{1,0:T(1,128)S(1)} %bitcast.3, ...), custom_call_target="tpu_custom_call" | custom-call | tf_op jit(solution)/shard_map/pallas_call | solution.py:323
  131.2 0.7 copy.21
  131.8 0.9 copy.22
  132.7 0.7 copy.23
Async XLA Ops:
  0.6 0.8 copy-start.9
  0.6 0.8 copy-start.8
  1.4 1.0 copy-start
  2.4 0.9 copy-start.1
  3.3 0.9 copy-start.2
  4.2 0.9 copy-start.3
  5.1 0.9 copy-start.4
  6.1 0.9 copy-start.5
  7.0 0.9 copy-start.6
  7.9 0.8 copy-start.7
  8.7 0.7 copy-start.10
  9.4 0.7 copy-start.11
  10.1 0.7 copy-start.12
  10.8 0.7 copy-start.13

commit v3 on v2

--- a/solution.py
+++ b/solution.py
@@ -2,7 +2,6 @@
 
 import jax
 import jax.numpy as jnp
-import ml_dtypes
 import numpy as np
 from jax import lax
 from jax.experimental import pallas as pl
@@ -18,6 +17,8 @@
 SIDE = 4
 LANES = 128
 CH = 8
+N_IN = 7
+VMEM_BYTES = 63 * 1024 * 1024
 
 
 def constants(blocks, width):
@@ -34,17 +35,14 @@
     f2 = np.block([[c, -s], [s, c]])
     g2 = np.block([[c, s], [-s, c]])
 
-    def split(m):
-        high = m.astype(ml_dtypes.bfloat16)
-        low = (m - high.astype(np.float64)).astype(ml_dtypes.bfloat16)
-        return high, low
-
-    f1h, f1l = split(f1)
-    f2h, f2l = split(f2)
-    g1h, g1l = split(g1)
-    g2h, g2l = split(g2)
-    twists = [np.cos(twist).astype(np.float32), np.sin(twist).astype(np.float32)]
-    return [np.concatenate([f1h, f1l], axis=0), f2h, f2l, g1h, g1l, g2h, g2l] + twists
+    pack = np.zeros((6 * width, 2 * width), np.float32)
+    pack[: 2 * width] = f2
+    pack[2 * width : 4 * width] = g2
+    pack[4 * width : 5 * width, :blocks] = f1
+    pack[5 * width : 5 * width + blocks, :width] = g1
+    pack[5 * width + blocks : 6 * width, :width] = np.cos(twist)
+    pack[5 * width + blocks : 6 * width, width:] = np.sin(twist)
+    return pack
 
 
 def dot(a, b):
@@ -57,13 +55,22 @@
 
 
 def kernel(
-    feat, taps, filt, skip, gain, grad,
-    f1, f2h, f2l, g1h, g1l, g2h, g2l, wr, wi,
-    out, fgrad, hgrad,
-    send, recv, qt, kt, vt, mt, st, it, gt, ct, spec_h, spec_x, spec_g, th, tl, db,
-    halo_s, halo_r, norm_s, norm_r,
-    send_sem, recv_sem, halo_send, halo_recv, norm_send, norm_recv,
+    *refs,
 ):
+    held, (out, fgrad, hgrad) = refs[:N_IN], refs[N_IN : N_IN + 3]
+    (send, recv, qt, kt, vt, st, it, gt, ct, spec_h, spec_x, spec_g, th, tl, db,
+     halo_s, halo_r, norm_s, norm_r,
+     f1, f2h, f2l, g1h, g1l, g2h, g2l, wr, wi,
+     send_sem, recv_sem, halo_send, halo_recv, norm_send, norm_recv, in_sem) = refs[N_IN + 3 : -N_IN]
+    local = refs[-N_IN:]
+    feat, taps, filt, skip, gain, grad, consts = local
+    fetch = [
+        pltpu.make_async_copy(held[i], local[i], in_sem.at[i]) for i in range(N_IN)
+    ]
+    early = (2, 0)
+    late = [i for i in range(N_IN) if i not in early]
+    for i in early:
+        fetch[i].start()
     me = lax.axis_index("context")
     lane = lax.axis_index("tensor")
     n_ctx = lax.axis_size("context")
@@ -73,6 +80,7 @@
     chunks = [slice(j * LANES, (j + 1) * LANES) for j in range(wide // LANES)]
 
     def peer(i):
+        i = n_ctx - i
         k = i // SIDE
         odd = k % 2
         dz = odd * ((k + 1) // 2) + (1 - odd) * (RING - k // 2)
@@ -92,6 +100,8 @@
 
     lax.fori_loop(1, n_ctx, greet, 0)
     lax.fori_loop(1, n_ten, greet_tensor, 0)
+    for i in late:
+        fetch[i].start()
 
     def tile(i):
         return pl.ds(pl.multiple_of(i * CH, CH), CH)
@@ -126,8 +136,10 @@
             device_id_type=MESH,
         )
 
+    fetch[2].wait()
     for j, c in enumerate(chunks):
         send[0, c, :] = filt[:, c].astype(F32).T
+    fetch[0].wait()
     for i in range(3):
         halo_s[0, 2 * i : 2 * i + 2, :] = feat[i, 112:128, :].astype(F32)[14:16]
     halo_s[0, 6:8, :] = jnp.zeros((2, wide), F32)
@@ -136,6 +148,14 @@
     first_halo = halo_copy(0, (me + 1) % n_ctx)
     first_halo.start()
     scatter(0)
+    for i in late:
+        fetch[i].wait()
+    f2h[...], f2l[...] = halves(consts[0:256, :])
+    g2h[...], g2l[...] = halves(consts[256:512, :])
+    f1[0:128, :], f1[128:256, :] = halves(consts[512:640, 0:64])
+    g1h[...], g1l[...] = halves(consts[640:704, 0:128])
+    wr[...] = consts[704:768, 0:128]
+    wi[...] = consts[704:768, 128:256]
 
     for j, c in enumerate(chunks):
         st[c, :] = (grad[:, c].astype(F32) * gain[0:1, c]).T
@@ -153,9 +173,9 @@
             x1 = jnp.where(row == 0, near, pltpu.roll(x, 1, 0))
             x2 = jnp.where(row == 0, far, jnp.where(row == 1, near, pltpu.roll(x, 2, 0)))
             parts.append(
-                taps[3 * i : 3 * i + 1, c] * x
-                + taps[3 * i + 1 : 3 * i + 2, c] * x1
-                + taps[3 * i + 2 : 3 * i + 3, c] * x2
+                taps[i, 0 : 1, c] * x
+                + taps[i, 1 : 2, c] * x1
+                + taps[i, 2 : 3, c] * x2
             )
         qt[c, :] = parts[0].T
         k, v = parts[1].T, parts[2].T
@@ -163,8 +183,6 @@
         vt[c, :] = v
         send[1, c, :] = (k * v).astype(BF16).astype(F32)
     scatter(1)
-    for j, c in enumerate(chunks):
-        mt[c, :] = send[1, c, :]
 
     blocks = 64
 
@@ -225,7 +243,7 @@
     square = jnp.zeros((1, LANES), F32)
     cross = jnp.zeros((1, LANES), F32)
     for c in chunks:
-        inner = recv[2, c, :] + gt[c, :] * mt[c, :]
+        inner = recv[2, c, :] + gt[c, :] * send[1, c, :]
         gated = qt[c, :] * inner
         it[c, :] = inner
         ct[c, :] = gated
@@ -296,9 +314,9 @@
                 jnp.where(row == LANES - 2, near, pltpu.roll(x, LANES - 2, 0)),
             )
             fgrad[i, :, c] = (
-                taps[3 * i : 3 * i + 1, c] * x
-                + taps[3 * i + 1 : 3 * i + 2, c] * x1
-                + taps[3 * i + 2 : 3 * i + 3, c] * x2
+                taps[i, 0 : 1, c] * x
+                + taps[i, 1 : 2, c] * x1
+                + taps[i, 2 : 3, c] * x2
             )
     arrived(5)
     for c in chunks:
@@ -313,27 +331,54 @@
     pltpu.make_async_copy(norm_r.at[spent], norm_r.at[spent], norm_send).wait()
 
 
+def deliver(a, b, c, a_out, b_out, c_out, a_mid, b_mid, c_mid, sem):
+    mids = (a_mid, b_mid, c_mid)
+    loads = [pltpu.make_async_copy(x, y, sem.at[i]) for i, (x, y) in enumerate(zip((a, b, c), mids))]
+    stores = [
+        pltpu.make_async_copy(x, y, sem.at[3 + i])
+        for i, (x, y) in enumerate(zip(mids, (a_out, b_out, c_out)))
+    ]
+    for load in loads:
+        load.start()
+    for load, store in zip(loads, stores):
+        load.wait()
+        store.start()
+    for store in stores:
+        store.wait()
+
+
 def per_device(features, short_filter, long_filter, skip_gain, norm_gain, out_grad):
     rows, wide = long_filter.shape
+    anywhere = pl.BlockSpec(memory_space=pl.ANY)
     vmem = pl.BlockSpec(memory_space=pltpu.VMEM)
     column = pltpu.VMEM((wide, rows), F32)
     spec = pltpu.VMEM((wide, 2 * rows), F32)
     half = pltpu.VMEM((wide, 2 * rows), BF16)
-    consts = [jnp.asarray(x) for x in constants(64, rows)]
-    out, fgrad, hgrad = pl.pallas_call(
+    consts = jnp.asarray(constants(64, rows))
+    operands = (
+        features,
+        short_filter,
+        long_filter,
+        skip_gain.reshape(1, wide),
+        norm_gain.reshape(1, wide),
+        out_grad,
+        consts,
+    )
+    shapes = (
+        jax.ShapeDtypeStruct((rows, wide), BF16),
+        jax.ShapeDtypeStruct((3, rows, wide), F32),
+        jax.ShapeDtypeStruct((rows, wide), F32),
+    )
+    results = pl.pallas_call(
         kernel,
-        out_shape=(
-            jax.ShapeDtypeStruct((rows, wide), BF16),
-            jax.ShapeDtypeStruct((3, rows, wide), F32),
-            jax.ShapeDtypeStruct((rows, wide), F32),
-        ),
-        in_specs=[vmem] * (6 + len(consts)),
+        out_shape=shapes,
+        in_specs=[anywhere] * N_IN,
         out_specs=[vmem] * 3,
         scratch_shapes=[
             pltpu.VMEM((6, wide, rows), F32),
             pltpu.VMEM((6, wide, rows), F32),
         ]
-        + [column] * 8
+        + [column] * 7
         + [spec] * 3
         + [half] * 2
         + [
@@ -342,26 +387,37 @@
             pltpu.VMEM((2, 8, wide), F32),
             pltpu.VMEM((8, rows), F32),
             pltpu.VMEM((8, 8, rows), F32),
+            pltpu.VMEM((256, 64), BF16),
+            pltpu.VMEM((256, 256), BF16),
+            pltpu.VMEM((256, 256), BF16),
+            pltpu.VMEM((64, 128), BF16),
+            pltpu.VMEM((64, 128), BF16),
+            pltpu.VMEM((256, 256), BF16),
+            pltpu.VMEM((256, 256), BF16),
+            pltpu.VMEM((64, 128), F32),
+            pltpu.VMEM((64, 128), F32),
             pltpu.SemaphoreType.DMA((6,)),
             pltpu.SemaphoreType.DMA((6,)),
             pltpu.SemaphoreType.DMA((2,)),
             pltpu.SemaphoreType.DMA((2,)),
             pltpu.SemaphoreType.DMA,
             pltpu.SemaphoreType.DMA,
-        ],
+            pltpu.SemaphoreType.DMA((N_IN,)),
+        ]
+        + [pltpu.VMEM(x.shape, x.dtype) for x in operands],
         compiler_params=pltpu.CompilerParams(
-            collective_id=0, has_side_effects=True, vmem_limit_bytes=48 * 1024 * 1024
+            collective_id=0, has_side_effects=True, vmem_limit_bytes=VMEM_BYTES
         ),
-    )(
-        features,
-        short_filter.reshape(9, wide),
-        long_filter,
-        skip_gain.reshape(1, wide),
-        norm_gain.reshape(1, wide),
-        out_grad,
-        *consts,
-    )
-    return out, fgrad, hgrad
+    )(*operands)
+    return pl.pallas_call(
+        deliver,
+        out_shape=shapes,
+        in_specs=[anywhere] * 3,
+        out_specs=[anywhere] * 3,
+        scratch_shapes=[pltpu.VMEM(x.shape, x.dtype) for x in shapes]
+        + [pltpu.SemaphoreType.DMA((6,))],
+        compiler_params=pltpu.CompilerParams(vmem_limit_bytes=VMEM_BYTES),
+    )(*results)
 
 
 def solution(mesh):

time: 134 us -> 109 us (0.81)
  the two profiles are of different devices: /device:TPU:32 before, /device:TPU:24 now
where the time goes in v3:
time: 109 us; the launch traced here: 108 us
  Pallas kernels  107 us (98%)
    pallas_call x1, Pallas kernels, per_device(): pl.pallas_call(kernel, out_shape=shapes, in_specs=[anywhere] * N_IN, out_...  105 us
    pallas_call x1, Pallas kernels, per_device(): pl.pallas_call(deliver, out_shape=shapes, in_specs=[anywhere] * 3, out_sp...  2.22 us

profile of v3, /device:TPU:24, one launch (start us, length us, event | category | flops | bytes accessed | tf_op | source)
XLA Modules:
  0.0 107.6 jit_solution(9597598275068104428)
XLA Ops:
  0.6 104.8 %shard_map.94 = (bf16[128,512]{1,0:T(8,128)(2,1)}, f32[3,128,512]{2,1,0:T(8,128)}, f32[128,512]{1,0:T(8,128)}) custom-call(bf16[3,128,512]{2,1,0:T(8,128)(2,1)} %refs_0_.1, f32[3,3,512]{2,1,0:T(4,128)} %refs_1_.1, bf16[128,512]{1,0:T(8,128)(2,1)} %refs_2_.1, f32[1,512]{1,0:T(1,128)} %bitcast.2, f32[1,512]{1,0:T(1,128)} %bitcast.3, bf16[128,512]{1,0:T(8,128)(2,1)} %refs_5_.1, ...), custom_call_target="tpu_custom_call" | custom-call | tf_op jit(solution)/shard_map/pallas_call | solution.py:372
  105.4 2.2 %shard_map.95 = (bf16[128,512]{1,0:T(8,128)(2,1)}, f32[3,128,512]{2,1,0:T(8,128)}, f32[128,512]{1,0:T(8,128)}) custom-call(bf16[128,512]{1,0:T(8,128)(2,1)} %get-tuple-element.6.a, f32[3,128,512]{2,1,0:T(8,128)} %get-tuple-element.7.b, f32[128,512]{1,0:T(8,128)} %get-tuple-element.8.c), custom_call_target="tpu_custom_call" | custom-call | tf_op jit(solution)/shard_map/pallas_call | solution.py:412

commit v4 on v3

--- a/solution.py
+++ b/solution.py
@@ -17,6 +17,7 @@
 SIDE = 4
 LANES = 128
 CH = 8
+HALF = CH // 2
 N_IN = 7
 VMEM_BYTES = 63 * 1024 * 1024
 
@@ -61,7 +62,8 @@
     (send, recv, qt, kt, vt, st, it, gt, ct, spec_h, spec_x, spec_g, th, tl, db,
      halo_s, halo_r, norm_s, norm_r,
      f1, f2h, f2l, g1h, g1l, g2h, g2l, wr, wi,
-     send_sem, recv_sem, halo_send, halo_recv, norm_send, norm_recv, in_sem) = refs[N_IN + 3 : -N_IN]
+     send_sem, recv_sem, halo_send, halo_recv, norm_send, norm_recv, in_sem, ring_sem,
+     out_v, fgrad_v, out_sem) = refs[N_IN + 3 : -N_IN]
     local = refs[-N_IN:]
     feat, taps, filt, skip, gain, grad, consts = local
     fetch = [
@@ -88,8 +90,9 @@
 
     barrier = pltpu.get_barrier_semaphore()
 
-    def greet(i, carry):
-        pl.semaphore_signal(barrier, inc=1, device_id={"context": peer(i)}, device_id_type=MESH)
+    def greet_z(i, carry):
+        p = ((my_z + i) % RING) * SIDE + my_y
+        pl.semaphore_signal(barrier, inc=1, device_id={"context": p}, device_id_type=MESH)
         return carry
 
     def greet_tensor(i, carry):
@@ -98,33 +101,58 @@
         )
         return carry
 
-    lax.fori_loop(1, n_ctx, greet, 0)
+    beside = [my_z * SIDE + (my_y + i) % SIDE for i in range(1, SIDE)]
+    lax.fori_loop(1, RING, greet_z, 0)
+    for p in beside:
+        pl.semaphore_signal(barrier, inc=1, device_id={"context": p}, device_id_type=MESH)
     lax.fori_loop(1, n_ten, greet_tensor, 0)
     for i in late:
         fetch[i].start()
 
-    def tile(i):
-        return pl.ds(pl.multiple_of(i * CH, CH), CH)
-
-    def scatter(u):
-        pltpu.make_async_copy(send.at[u, tile(me)], recv.at[u, tile(me)], recv_sem.at[u]).start()
-
-        def body(i, carry):
-            p = peer(i)
+    def piece(i, part):
+        if part is None:
+            return pl.ds(pl.multiple_of(i * CH, CH), CH)
+        return pl.ds(pl.multiple_of(i * CH + part * HALF, HALF), HALF)
+
+    def scatter(u, part=None, land=None, even_first=False):
+        slot = 2 * u + (part or 0)
+        land = recv.at[u] if land is None else land
+        mine = piece(me, part)
+        pltpu.make_async_copy(send.at[u, mine], land.at[mine], recv_sem.at[slot]).start()
+
+        def push(p):
             pltpu.make_async_remote_copy(
-                src_ref=send.at[u, tile(p)],
-                dst_ref=recv.at[u, tile(me)],
+                src_ref=send.at[u, piece(p, part)],
+                dst_ref=land.at[mine],
                 send_sem=send_sem.at[u],
-                recv_sem=recv_sem.at[u],
+                recv_sem=recv_sem.at[slot],
                 device_id={"context": p},
                 device_id_type=MESH,
             ).start()
+
+        def body(i, carry):
+            push(peer(i))
             return carry
 
-        lax.fori_loop(1, n_ctx, body, 0)
-
-    def arrived(u):
-        pltpu.make_async_copy(send.at[u], recv.at[u], recv_sem.at[u]).wait()
+        if not even_first:
+            lax.fori_loop(1, n_ctx, body, 0)
+            return
+        same = my_z % 2
+        for odd, count in ((same, 31 + same), (1 - same, 32 - same)):
+
+            def by_parity(i, carry, odd=odd):
+                j = i // SIDE
+                dz = (8 - odd - 2 * ((j + 1 - odd) // 2)) * (2 * ((j + odd) % 2) - 1)
+                push(((my_z + dz + RING) % RING) * SIDE + (my_y + i + 1) % SIDE)
+                return carry
+
+            lax.fori_loop(0, count, by_parity, 0)
+
+    def arrived(u, part=None, land=None):
+        slot = 2 * u + (part or 0)
+        land = recv.at[u] if land is None else land
+        size = pl.ds(0, n_ctx * (CH if part is None else HALF))
+        pltpu.make_async_copy(send.at[u, size], land.at[size], recv_sem.at[slot]).wait()
 
     def halo_copy(h, to):
         return pltpu.make_async_remote_copy(
@@ -143,7 +171,10 @@
     for i in range(3):
         halo_s[0, 2 * i : 2 * i + 2, :] = feat[i, 112:128, :].astype(F32)[14:16]
     halo_s[0, 6:8, :] = jnp.zeros((2, wide), F32)
-    pl.semaphore_wait(barrier, n_ctx - 1 + n_ten - 1)
+    pl.semaphore_wait(barrier, RING - 1 + SIDE - 1 + n_ten - 1)
+    for p in beside:
+        pl.semaphore_signal(ring_sem, inc=1, device_id={"context": p}, device_id_type=MESH)
+    pl.semaphore_wait(ring_sem, SIDE - 1)
 
     first_halo = halo_copy(0, (me + 1) % n_ctx)
     first_halo.start()
@@ -182,12 +213,13 @@
         kt[c, :] = k
         vt[c, :] = v
         send[1, c, :] = (k * v).astype(BF16).astype(F32)
-    scatter(1)
+    scatter(1, 0)
+    scatter(1, 1)
 
     blocks = 64
 
-    def forward(u, spec):
-        for p in range(CH // 2):
+    def forward(u, spec, part):
+        for p in range(part * HALF // 2, (part + 1) * HALF // 2):
             x = jnp.concatenate(
                 [recv[u, pl.ds(2 * p + e, blocks, stride=CH), :] for e in range(2)], axis=1
             ).astype(BF16)
@@ -203,10 +235,11 @@
                 h, l = halves(im * wr[...] - re * wi[...])
                 th[rows, LANES:] = h
                 tl[rows, LANES:] = l
-        spec[...] = dot(th[...], f2h[...]) + dot(tl[...], f2h[...]) + dot(th[...], f2l[...])
-
-    def inverse(a, b, sign, u):
-        for p in range(CH // 2):
+        rows = slice(part * HALF * blocks, (part + 1) * HALF * blocks)
+        spec[rows, :] = dot(th[rows, :], f2h[...]) + dot(tl[rows, :], f2h[...]) + dot(th[rows, :], f2l[...])
+
+    def inverse(a, b, sign, u, part):
+        for p in range(part * HALF // 2, (part + 1) * HALF // 2):
             rows = slice(2 * p * blocks, 2 * (p + 1) * blocks)
             ar, ai = a[rows, :LANES], a[rows, LANES:]
             br, bi = b[rows, :LANES], sign * b[rows, LANES:]
@@ -216,11 +249,13 @@
             h, l = halves(ar * bi + ai * br)
             th[rows, LANES:] = h
             tl[rows, LANES:] = l
-        t = dot(th[...], g2h[...]) + dot(tl[...], g2h[...]) + dot(th[...], g2l[...])
-        for p in range(CH // 2):
+        base = part * HALF * blocks
+        rows = slice(base, base + HALF * blocks)
+        t = dot(th[rows, :], g2h[...]) + dot(tl[rows, :], g2h[...]) + dot(th[rows, :], g2l[...])
+        for p in range(part * HALF // 2, (part + 1) * HALF // 2):
             both = []
             for e in range(2):
-                rows = slice((2 * p + e) * blocks, (2 * p + e + 1) * blocks)
+                rows = slice((2 * p + e) * blocks - base, (2 * p + e + 1) * blocks - base)
                 re, im = t[rows, :LANES], t[rows, LANES:]
                 both.append(
                     jnp.concatenate(
@@ -233,13 +268,16 @@
                 send[u, pl.ds(2 * p + e, blocks, stride=CH), :] = y[:, e * LANES : (e + 1) * LANES]
 
     arrived(0)
-    forward(0, spec_h)
-    arrived(1)
-    forward(1, spec_x)
-    inverse(spec_x, spec_h, 1.0, 2)
-    scatter(2)
-
-    arrived(2)
+    for part in range(2):
+        forward(0, spec_h, part)
+    for part in range(2):
+        arrived(1, part)
+        forward(1, spec_x, part)
+        inverse(spec_x, spec_h, 1.0, 2, part)
+        scatter(2, part, even_first=True)
+
+    for part in range(2):
+        arrived(2, part)
     square = jnp.zeros((1, LANES), F32)
     cross = jnp.zeros((1, LANES), F32)
     for c in chunks:
@@ -278,19 +316,23 @@
         send[3, c, :] = d_conv.astype(BF16).astype(F32)
         gt[c, :] = gt[c, :] * d_conv
         it[c, :] = d_gated * it[c, :]
-    scatter(3)
+    scatter(3, 0)
+    scatter(3, 1)
     for c in chunks:
-        out[:, c] = ((ct[c, :] * scale).T * gain[0:1, c]).astype(BF16)
+        out_v[:, c] = ((ct[c, :] * scale).T * gain[0:1, c]).astype(BF16)
         db[0, :, c] = it[c, :].T
 
-    arrived(3)
-    forward(3, spec_g)
-    inverse(spec_g, spec_h, -1.0, 4)
-    scatter(4)
-    inverse(spec_g, spec_x, -1.0, 5)
-    scatter(5)
-
-    arrived(4)
+    out_copy = pltpu.make_async_copy(out_v, out, out_sem.at[0])
+    out_copy.start()
+    for part in range(2):
+        arrived(3, part)
+        forward(3, spec_g, part)
+        inverse(spec_g, spec_h, -1.0, 4, part)
+        scatter(4, part)
+        inverse(spec_g, spec_x, -1.0, 5, part)
+    scatter(5, land=hgrad)
+    for part in range(2):
+        arrived(4, part)
     for c in chunks:
         d_mixed = recv[4, c, :] + gt[c, :]
         db[1, :, c] = (d_mixed * vt[c, :]).T
@@ -313,14 +355,16 @@
                 far,
                 jnp.where(row == LANES - 2, near, pltpu.roll(x, LANES - 2, 0)),
             )
-            fgrad[i, :, c] = (
+            fgrad_v[i, :, c] = (
                 taps[i, 0 : 1, c] * x
                 + taps[i, 1 : 2, c] * x1
                 + taps[i, 2 : 3, c] * x2
             )
-    arrived(5)
-    for c in chunks:
-        hgrad[:, c] = recv[5, c, :].T
+    fgrad_copy = pltpu.make_async_copy(fgrad_v, fgrad, out_sem.at[1])
+    fgrad_copy.start()
+    arrived(5, land=hgrad)
+    out_copy.wait()
+    fgrad_copy.wait()
 
     for u in range(6):
         gone = pl.ds(0, (n_ctx - 1) * CH)
@@ -331,17 +375,22 @@
     pltpu.make_async_copy(norm_r.at[spent], norm_r.at[spent], norm_send).wait()
 
 
-def deliver(a, b, c, a_out, b_out, c_out, a_mid, b_mid, c_mid, sem):
-    mids = (a_mid, b_mid, c_mid)
-    loads = [pltpu.make_async_copy(x, y, sem.at[i]) for i, (x, y) in enumerate(zip((a, b, c), mids))]
+def deliver(a, b, c, a_out, b_out, c_out, a_mid, b_mid, c_mid, c_turned, sem):
+    loads = [
+        pltpu.make_async_copy(x, y, sem.at[i])
+        for i, (x, y) in enumerate(((c, c_mid), (b, b_mid), (a, a_mid)))
+    ]
     stores = [
         pltpu.make_async_copy(x, y, sem.at[3 + i])
-        for i, (x, y) in enumerate(zip(mids, (a_out, b_out, c_out)))
+        for i, (x, y) in enumerate(((c_turned, c_out), (b_mid, b_out), (a_mid, a_out)))
     ]
     for load in loads:
         load.start()
     for load, store in zip(loads, stores):
         load.wait()
+        if load is loads[0]:
+            for j in range(0, c_mid.shape[0], LANES):
+                c_turned[:, j : j + LANES] = c_mid[j : j + LANES, :].T
         store.start()
     for store in stores:
         store.wait()
@@ -350,7 +399,6 @@
 def per_device(features, short_filter, long_filter, skip_gain, norm_gain, out_grad):
     rows, wide = long_filter.shape
     anywhere = pl.BlockSpec(memory_space=pl.ANY)
-    vmem = pl.BlockSpec(memory_space=pltpu.VMEM)
     column = pltpu.VMEM((wide, rows), F32)
     spec = pltpu.VMEM((wide, 2 * rows), F32)
     half = pltpu.VMEM((wide, 2 * rows), BF16)
@@ -369,11 +417,12 @@
         jax.ShapeDtypeStruct((3, rows, wide), F32),
         jax.ShapeDtypeStruct((rows, wide), F32),
     )
+    column_grad = jax.ShapeDtypeStruct((wide, rows), F32)
     results = pl.pallas_call(
         kernel,
-        out_shape=shapes,
+        out_shape=shapes[:2] + (column_grad,),
         in_specs=[anywhere] * N_IN,
-        out_specs=[vmem] * 3,
+        out_specs=[anywhere] * 3,
         scratch_shapes=[
             pltpu.VMEM((6, wide, rows), F32),
             pltpu.VMEM((6, wide, rows), F32),
@@ -397,12 +446,16 @@
             pltpu.VMEM((64, 128), F32),
             pltpu.VMEM((64, 128), F32),
             pltpu.SemaphoreType.DMA((6,)),
-            pltpu.SemaphoreType.DMA((6,)),
+            pltpu.SemaphoreType.DMA((12,)),
             pltpu.SemaphoreType.DMA((2,)),
             pltpu.SemaphoreType.DMA((2,)),
             pltpu.SemaphoreType.DMA,
             pltpu.SemaphoreType.DMA,
             pltpu.SemaphoreType.DMA((N_IN,)),
+            pltpu.SemaphoreType.REGULAR,
+            pltpu.VMEM((rows, wide), BF16),
+            pltpu.VMEM((3, rows, wide), F32),
+            pltpu.SemaphoreType.DMA((2,)),
         ]
         + [pltpu.VMEM(x.shape, x.dtype) for x in operands],
         compiler_params=pltpu.CompilerParams(
@@ -414,7 +467,7 @@
         out_shape=shapes,
         in_specs=[anywhere] * 3,
         out_specs=[anywhere] * 3,
-        scratch_shapes=[pltpu.VMEM(x.shape, x.dtype) for x in shapes]
+        scratch_shapes=[pltpu.VMEM(x.shape, x.dtype) for x in shapes[:2] + (column_grad, shapes[2])]
         + [pltpu.SemaphoreType.DMA((6,))],
         compiler_params=pltpu.CompilerParams(vmem_limit_bytes=VMEM_BYTES),
     )(*results)

time: 109 us -> 102 us (0.936)
  Pallas kernels: 107 us -> 101 us
    pallas_call x1, Pallas kernels: 105 us -> 98.6 us  [per_device(): pl.pallas_call(kernel, out_shape=shapes[:2] + (column_grad,), in_specs=[a...]
where the time goes in v4:
time: 102 us; the launch traced here: 101 us
  Pallas kernels  101 us (99%)
    pallas_call x1, Pallas kernels, per_device(): pl.pallas_call(kernel, out_shape=shapes[:2] + (column_grad,), in_specs=[a...  98.6 us
    pallas_call x1, Pallas kernels, per_device(): pl.pallas_call(deliver, out_shape=shapes, in_specs=[anywhere] * 3, out_sp...  2.18 us

profile of v4, /device:TPU:24, one launch (start us, length us, event | category | flops | bytes accessed | tf_op | source)
XLA Modules:
  0.0 101.4 jit_solution(8580409200018924118)
XLA Ops:
  0.6 98.6 %shard_map.94 = (bf16[128,512]{1,0:T(8,128)(2,1)}, f32[3,128,512]{2,1,0:T(8,128)}, f32[512,128]{1,0:T(8,128)}) custom-call(bf16[3,128,512]{2,1,0:T(8,128)(2,1)} %refs_0_.1, f32[3,3,512]{2,1,0:T(4,128)} %refs_1_.1, bf16[128,512]{1,0:T(8,128)(2,1)} %refs_2_.1, f32[1,512]{1,0:T(1,128)} %bitcast.2, f32[1,512]{1,0:T(1,128)} %bitcast.3, bf16[128,512]{1,0:T(8,128)(2,1)} %refs_5_.1, ...), custom_call_target="tpu_custom_call" | custom-call | tf_op jit(solution)/shard_map/pallas_call | solution.py:421
  99.2 2.2 %shard_map.95 = (bf16[128,512]{1,0:T(8,128)(2,1)}, f32[3,128,512]{2,1,0:T(8,128)}, f32[128,512]{1,0:T(8,128)}) custom-call(bf16[128,512]{1,0:T(8,128)(2,1)} %get-tuple-element.6.a, f32[3,128,512]{2,1,0:T(8,128)} %get-tuple-element.7.b, f32[512,128]{1,0:T(8,128)} %get-tuple-element.8.c), custom_call_target="tpu_custom_call" | custom-call | tf_op jit(solution)/shard_map/pallas_call | solution.py:465

commit v5 on v4

--- a/solution.py
+++ b/solution.py
@@ -81,12 +81,14 @@
     wide = LANES * SIDE
     chunks = [slice(j * LANES, (j + 1) * LANES) for j in range(wide // LANES)]
 
-    def peer(i):
-        i = n_ctx - i
-        k = i // SIDE
-        odd = k % 2
-        dz = odd * ((k + 1) // 2) + (1 - odd) * (RING - k // 2)
-        return ((my_z + dz) % RING) * SIDE + (my_y + i % SIDE) % SIDE
+    columns = [(my_y + i) % SIDE for i in (2, 1, 3, 0)]
+
+    def ring_row(j):
+        k = RING - 1 - j
+        odd = (k + lane) % 2
+        m = k // 2 + k % 2
+        dz = odd * m + (1 - odd) * (RING - m)
+        return ((my_z + dz) % RING) * SIDE
 
     barrier = pltpu.get_barrier_semaphore()
 
@@ -114,7 +116,7 @@
             return pl.ds(pl.multiple_of(i * CH, CH), CH)
         return pl.ds(pl.multiple_of(i * CH + part * HALF, HALF), HALF)
 
-    def scatter(u, part=None, land=None, even_first=False):
+    def scatter(u, part=None, land=None, first=0):
         slot = 2 * u + (part or 0)
         land = recv.at[u] if land is None else land
         mine = piece(me, part)
@@ -130,23 +132,41 @@
                 device_id_type=MESH,
             ).start()
 
-        def body(i, carry):
-            push(peer(i))
+        def body(j, carry):
+            row = ring_row(j)
+            if first:
+
+                @pl.when(row >= first * SIDE)
+                def _():
+                    for y in columns:
+                        push(row + y)
+
+            else:
+                for y in columns:
+                    push(row + y)
             return carry
 
-        if not even_first:
-            lax.fori_loop(1, n_ctx, body, 0)
-            return
-        same = my_z % 2
-        for odd, count in ((same, 31 + same), (1 - same, 32 - same)):
-
-            def by_parity(i, carry, odd=odd):
-                j = i // SIDE
-                dz = (8 - odd - 2 * ((j + 1 - odd) // 2)) * (2 * ((j + odd) % 2) - 1)
-                push(((my_z + dz + RING) % RING) * SIDE + (my_y + i + 1) % SIDE)
-                return carry
-
-            lax.fori_loop(0, count, by_parity, 0)
+        def ahead(i, carry):
+            row = ((i + my_z) % first) * SIDE
+            for y in columns:
+
+                @pl.when(row + y != me)
+                def _():
+                    push(row + y)
+
+            return carry
+
+        def own_row():
+            for y in columns[:-1]:
+                push(my_z * SIDE + y)
+
+        if first:
+            lax.fori_loop(0, first, ahead, 0)
+        lax.fori_loop(0, RING - 1, body, 0)
+        if first:
+            pl.when(my_z >= first)(own_row)
+        else:
+            own_row()
 
     def arrived(u, part=None, land=None):
         slot = 2 * u + (part or 0)
@@ -274,7 +294,7 @@
         arrived(1, part)
         forward(1, spec_x, part)
         inverse(spec_x, spec_h, 1.0, 2, part)
-        scatter(2, part, even_first=True)
+        scatter(2, part)
 
     for part in range(2):
         arrived(2, part)
@@ -287,7 +307,6 @@
         ct[c, :] = gated
         square = square + jnp.sum(gated * gated, axis=0, keepdims=True)
         cross = cross + jnp.sum(st[c, :] * gated, axis=0, keepdims=True)
-    norm_s[...] = jnp.zeros((8, LANES), F32)
     norm_s[0:1, :] = square
     norm_s[1:2, :] = cross
     pltpu.make_async_copy(norm_s, norm_r.at[lane], norm_recv).start()
@@ -312,12 +331,13 @@
     pull = scale * scale * scale * (total[1:2] / CHANNELS)
     for c in chunks:
         d_gated = scale * st[c, :] - ct[c, :] * pull
-        d_conv = d_gated * qt[c, :]
-        send[3, c, :] = d_conv.astype(BF16).astype(F32)
-        gt[c, :] = gt[c, :] * d_conv
-        it[c, :] = d_gated * it[c, :]
+        send[3, c, :] = (d_gated * qt[c, :]).astype(BF16).astype(F32)
     scatter(3, 0)
     scatter(3, 1)
+    for c in chunks:
+        d_gated = scale * st[c, :] - ct[c, :] * pull
+        gt[c, :] = gt[c, :] * (d_gated * qt[c, :])
+        it[c, :] = d_gated * it[c, :]
     for c in chunks:
         out_v[:, c] = ((ct[c, :] * scale).T * gain[0:1, c]).astype(BF16)
         db[0, :, c] = it[c, :].T
@@ -330,7 +350,7 @@
         inverse(spec_g, spec_h, -1.0, 4, part)
         scatter(4, part)
         inverse(spec_g, spec_x, -1.0, 5, part)
-    scatter(5, land=hgrad)
+    scatter(5, land=hgrad, first=4)
     for part in range(2):
         arrived(4, part)
     for c in chunks:
@@ -434,8 +454,8 @@
             pltpu.VMEM((3, rows, wide), F32),
             pltpu.VMEM((2, 8, wide), F32),
             pltpu.VMEM((2, 8, wide), F32),
-            pltpu.VMEM((8, rows), F32),
-            pltpu.VMEM((8, 8, rows), F32),
+            pltpu.VMEM((2, rows), F32),
+            pltpu.VMEM((8, 2, rows), F32),
             pltpu.VMEM((256, 64), BF16),
             pltpu.VMEM((256, 256), BF16),
             pltpu.VMEM((256, 256), BF16),

time: 102 us -> 99 us (0.971)
  Pallas kernels: 101 us -> 97.8 us
    pallas_call x1, Pallas kernels: 98.6 us -> 95.6 us  [per_device(): pl.pallas_call(kernel, out_shape=shapes[:2] + (column_grad,), in_specs=[a...]
where the time goes in v5:
time: 99 us; the launch traced here: 98.5 us
  Pallas kernels  97.8 us (99%)
    pallas_call x1, Pallas kernels, per_device(): pl.pallas_call(kernel, out_shape=shapes[:2] + (column_grad,), in_specs=[a...  95.6 us
    pallas_call x1, Pallas kernels, per_device(): pl.pallas_call(deliver, out_shape=shapes, in_specs=[anywhere] * 3, out_sp...  2.18 us

profile of v5, /device:TPU:24, one launch (start us, length us, event | category | flops | bytes accessed | tf_op | source)
XLA Modules:
  0.0 98.5 jit_solution(11645009542554473552)
XLA Ops:
  0.6 95.6 %shard_map.94 = (bf16[128,512]{1,0:T(8,128)(2,1)}, f32[3,128,512]{2,1,0:T(8,128)}, f32[512,128]{1,0:T(8,128)}) custom-call(bf16[3,128,512]{2,1,0:T(8,128)(2,1)} %refs_0_.1, f32[3,3,512]{2,1,0:T(4,128)} %refs_1_.1, bf16[128,512]{1,0:T(8,128)(2,1)} %refs_2_.1, f32[1,512]{1,0:T(1,128)} %bitcast.2, f32[1,512]{1,0:T(1,128)} %bitcast.3, bf16[128,512]{1,0:T(8,128)(2,1)} %refs_5_.1, ...), custom_call_target="tpu_custom_call" | custom-call | tf_op jit(solution)/shard_map/pallas_call | solution.py:441
  96.3 2.2 %shard_map.95 = (bf16[128,512]{1,0:T(8,128)(2,1)}, f32[3,128,512]{2,1,0:T(8,128)}, f32[128,512]{1,0:T(8,128)}) custom-call(bf16[128,512]{1,0:T(8,128)(2,1)} %get-tuple-element.6.a, f32[3,128,512]{2,1,0:T(8,128)} %get-tuple-element.7.b, f32[512,128]{1,0:T(8,128)} %get-tuple-element.8.c), custom_call_target="tpu_custom_call" | custom-call | tf_op jit(solution)/shard_map/pallas_call | solution.py:485

commit v6 on v5

--- a/solution.py
+++ b/solution.py
@@ -303,7 +303,6 @@
     for c in chunks:
         inner = recv[2, c, :] + gt[c, :] * send[1, c, :]
         gated = qt[c, :] * inner
-        it[c, :] = inner
         ct[c, :] = gated
         square = square + jnp.sum(gated * gated, axis=0, keepdims=True)
         cross = cross + jnp.sum(st[c, :] * gated, axis=0, keepdims=True)
@@ -311,7 +310,7 @@
     norm_s[1:2, :] = cross
     pltpu.make_async_copy(norm_s, norm_r.at[lane], norm_recv).start()
 
-    def share(i, carry):
+    for i in (4, 5, 3, 6, 2, 7, 1):
         pltpu.make_async_remote_copy(
             src_ref=norm_s,
             dst_ref=norm_r.at[lane],
@@ -320,9 +319,6 @@
             device_id={"tensor": (lane + i) % n_ten},
             device_id_type=MESH,
         ).start()
-        return carry
-
-    lax.fori_loop(1, n_ten, share, 0)
     pltpu.make_async_copy(norm_r, norm_r, norm_recv).wait()
     total = norm_r[0]
     for i in range(1, 8):
@@ -336,8 +332,8 @@
     scatter(3, 1)
     for c in chunks:
         d_gated = scale * st[c, :] - ct[c, :] * pull
+        it[c, :] = d_gated * (recv[2, c, :] + gt[c, :] * send[1, c, :])
         gt[c, :] = gt[c, :] * (d_gated * qt[c, :])
-        it[c, :] = d_gated * it[c, :]
     for c in chunks:
         out_v[:, c] = ((ct[c, :] * scale).T * gain[0:1, c]).astype(BF16)
         db[0, :, c] = it[c, :].T

time: 99 us -> 98.9 us (level)
  no operation moved by 1% of the time
where the time goes in v6:
time: 98.9 us; the launch traced here: 98.4 us
  Pallas kernels  97.8 us (99%)
    pallas_call x1, Pallas kernels, per_device(): pl.pallas_call(kernel, out_shape=shapes[:2] + (column_grad,), in_specs=[a...  95.6 us
    pallas_call x1, Pallas kernels, per_device(): pl.pallas_call(deliver, out_shape=shapes, in_specs=[anywhere] * 3, out_sp...  2.18 us

profile of v6, /device:TPU:24, one launch (start us, length us, event | category | flops | bytes accessed | tf_op | source)
XLA Modules:
  0.0 98.4 jit_solution(16759803144064372295)
XLA Ops:
  0.6 95.6 %shard_map.94 = (bf16[128,512]{1,0:T(8,128)(2,1)}, f32[3,128,512]{2,1,0:T(8,128)}, f32[512,128]{1,0:T(8,128)}) custom-call(bf16[3,128,512]{2,1,0:T(8,128)(2,1)} %refs_0_.1, f32[3,3,512]{2,1,0:T(4,128)} %refs_1_.1, bf16[128,512]{1,0:T(8,128)(2,1)} %refs_2_.1, f32[1,512]{1,0:T(1,128)} %bitcast.2, f32[1,512]{1,0:T(1,128)} %bitcast.3, bf16[128,512]{1,0:T(8,128)(2,1)} %refs_5_.1, ...), custom_call_target="tpu_custom_call" | custom-call | tf_op jit(solution)/shard_map/pallas_call | solution.py:437
  96.2 2.2 %shard_map.95 = (bf16[128,512]{1,0:T(8,128)(2,1)}, f32[3,128,512]{2,1,0:T(8,128)}, f32[128,512]{1,0:T(8,128)}) custom-call(bf16[128,512]{1,0:T(8,128)(2,1)} %get-tuple-element.6.a, f32[3,128,512]{2,1,0:T(8,128)} %get-tuple-element.7.b, f32[512,128]{1,0:T(8,128)} %get-tuple-element.8.c), custom_call_target="tpu_custom_call" | custom-call | tf_op jit(solution)/shard_map/pallas_call | solution.py:481
